TPU v7x, 32 devices: a whole 2x2x4 slice. The times are simulated.
32 devices in a mesh: row: 4 (over y, x), col: 8 (over z, core).
Axes of the slice: x: 2, y: 2, z: 4, core: 2. Of those that a mesh axis runs over, the one named last changes fastest.
Arguments:
- query: bfloat16 [1024, 1024], P(('row', 'col')), may hold values from -0.5375 to 0.5375
- passage: bfloat16 [1024, 1024], P(('row', 'col')), may hold values from -0.43 to 0.43
- positive: int32 [32, 32], P(('row', 'col')), may hold values from 0 to 31, each once within a row
Outputs:
- loss_value: float32 [], replicated
- grad_query: bfloat16 [1024, 1024], P(('row', 'col'))
- grad_passage: bfloat16 [1024, 1024], P(('row', 'col'))
Inputs may be any that keep to these rules, and one draw needn't show every extreme that they name: Each row of positive names every position 0 to 31 once.
All inputs are finite; a program needn't handle non-finite values.
Results may differ from a plain program's by a relative error of at most 0.015.
Values may be sent and summed in bfloat16 or wider, within the bound.
A program may use at most 64 MiB of HBM per device.

v0:
```python
import jax
import jax.numpy as jnp
from jax import lax
from jax.sharding import PartitionSpec as P

logit_scale = 20.0


def tile_scores(query_rows, passage_rows):
    return logit_scale * lax.dot_general(
        query_rows, passage_rows, (((1,), (1,)), ((), ())), preferred_element_type=jnp.float32
    )


def local(query, passage, positive):
    shard_rows = query.shape[0]
    row_devices = lax.axis_size("row")
    col_devices = lax.axis_size("col")
    passage_all = lax.all_gather(passage, "row", axis=0, tiled=True)
    query_all = lax.all_gather(query, "col", axis=0, tiled=True)
    scores = tile_scores(query_all, passage_all)
    row_local_peak = scores.max(axis=1)
    col_local_peak = scores.max(axis=0)
    row_peak = lax.pmax(row_local_peak, "col")
    col_peak = lax.pmax(col_local_peak, "row")
    row_sum = lax.psum(jnp.exp(scores - row_peak[:, None]).sum(axis=1), "col")
    col_sum = lax.psum(jnp.exp(scores - col_peak[None, :]).sum(axis=0), "row")
    row_lse = row_peak + jnp.log(row_sum)
    col_lse = col_peak + jnp.log(col_sum)
    weights = (
        0.5 * (jnp.exp(scores - row_lse[:, None]) + jnp.exp(scores - col_lse[None, :]))
    ).astype(jnp.bfloat16)
    query_sum = lax.psum_scatter(
        jnp.dot(weights, passage_all, preferred_element_type=jnp.float32).astype(jnp.bfloat16),
        "col",
        scatter_dimension=0,
        tiled=True,
    ).astype(jnp.float32)
    passage_sum = lax.psum_scatter(
        lax.dot_general(
            weights, query_all, (((0,), (0,)), ((), ())), preferred_element_type=jnp.float32
        ).astype(jnp.bfloat16),
        "row",
        scatter_dimension=0,
        tiled=True,
    ).astype(jnp.float32)
    slot_index = jnp.arange(shard_rows, dtype=jnp.int32)
    onehot = (positive[0][:, None] == slot_index[None, :]).astype(jnp.bfloat16)
    paired_passage = jnp.dot(onehot, passage, preferred_element_type=jnp.float32)
    paired_query = lax.dot_general(
        onehot, query, (((0,), (0,)), ((), ())), preferred_element_type=jnp.float32
    )
    positive_score = logit_scale * jnp.sum(query.astype(jnp.float32) * paired_passage, axis=1)
    grad_query = (logit_scale * (query_sum - paired_passage)).astype(jnp.bfloat16)
    grad_passage = (logit_scale * (passage_sum - paired_query)).astype(jnp.bfloat16)
    row_part = lax.dynamic_slice_in_dim(row_lse, lax.axis_index("col") * shard_rows, shard_rows)
    col_part = lax.dynamic_slice_in_dim(col_lse, lax.axis_index("row") * shard_rows, shard_rows)
    local_terms = jnp.sum(row_part) + jnp.sum(col_part) - 2.0 * jnp.sum(positive_score)
    summed = lax.psum(local_terms, ("row", "col"))
    loss_value = summed / (2.0 * shard_rows * row_devices * col_devices)
    return (loss_value, grad_query, grad_passage)


def solution(mesh):
    return jax.shard_map(
        local,
        mesh=mesh,
        in_specs=(P(("row", "col"), None), P(("row", "col"), None), P(("row", "col"), None)),
        out_specs=(P(), P(("row", "col"), None), P(("row", "col"), None)),
        check_vma=False,
    )
```

profile of v0, /device:TPU:0, one launch (start us, length us, event | category | flops | bytes accessed | tf_op | source)
XLA Modules:
  0.0 184.1 jit_solution(18403964406997825081)
XLA Ops:
  7.2 0.0 copy-start
  7.2 0.0 reduce-scatter.3.cloned.1.call-start
  7.2 10.7 %all_gather.7 = bf16[128,1024]{1,0:T(8,128)(2,1)S(1)} all-gather(bf16[32,1024]{1,0:T(8,128)(2,1)} %param.4), channel_id=1, replica_groups=mesh['row'=4,'col'=8] {'row'}, dimensions={0}, use_global_device_ids=true | all-gather | bytes 327680 | tf_op jit(solution)/shard_map/all_gather | solution.py:19
  17.9 0.0 copy-done
  17.9 15.4 %all_gather.6 = bf16[256,1024]{1,0:T(8,128)(2,1)S(1)} all-gather(bf16[32,1024]{1,0:T(8,128)(2,1)S(1)} %copy-done), channel_id=1, replica_groups=mesh['row'=4,'col'=8] {'col'}, dimensions={0}, use_global_device_ids=true | all-gather | bytes 589824 | tf_op jit(solution)/shard_map/all_gather | solution.py:20
  33.4 0.4 fusion.5
  33.7 8.9 %pmax.15 = f32[128]{0:T(128)S(1)} all-reduce(f32[128]{0:T(128)S(1)} %get-tuple-element.5), channel_id=1, replica_groups=mesh['row'=4,'col'=8] {'row'}, use_global_device_ids=true, to_apply=%region_6.0 | all-reduce | flops 128 | bytes 1024 | tf_op jit(solution)/shard_map/pmax | solution.py:25
  42.7 14.6 %pmax.14 = f32[256]{0:T(256)S(1)} all-reduce(f32[256]{0:T(256)S(1)} %get-tuple-element.6), channel_id=1, replica_groups=mesh['row'=4,'col'=8] {'col'}, use_global_device_ids=true, to_apply=%region_1.0 | all-reduce | flops 256 | bytes 2048 | tf_op jit(solution)/shard_map/pmax | solution.py:24
  57.3 0.2 exponential_reduce_fusion
  57.5 8.6 %psum.22 = f32[128]{0:T(128)S(1)} all-reduce(f32[128]{0:T(128)S(1)} %get-tuple-element.3), channel_id=1, replica_groups=mesh['row'=4,'col'=8] {'row'}, use_global_device_ids=true, to_apply=%region_8.0 | all-reduce | flops 128 | bytes 1024 | tf_op jit(solution)/shard_map/psum | solution.py:27
  66.1 13.6 %psum.21 = f32[256]{0:T(256)S(1)} all-reduce(f32[256]{0:T(256)S(1)} %get-tuple-element.4), channel_id=1, replica_groups=mesh['row'=4,'col'=8] {'col'}, use_global_device_ids=true, to_apply=%region_3.0 | all-reduce | flops 256 | bytes 2048 | tf_op jit(solution)/shard_map/psum | solution.py:26
  79.7 1.1 convolution_convert_fusion
  80.9 0.0 reduce-scatter.3.cloned.1.call-update
  80.9 0.0 reduce-scatter.5.cloned.1.call-start
  80.9 1.1 convolution_convert_fusion.1
  82.0 0.0 copy-start.1
  82.0 0.0 reduce-scatter.5.cloned.1.call-update
  82.0 0.7 dynamic-slice_reduce_fusion
  82.7 0.7 dynamic-slice_reduce_fusion.1
  84.7 0.0 copy-start.2
  84.7 24.6 %reduce-scatter.3.cloned.1.call-done = bf16[32,1024]{1,0:T(8,128)(2,1)} async-done(((bf16[256,1024]{1,0:T(8,128)(2,1)}), bf16[32,1024]{1,0:T(8,128)(2,1)}) %reduce-scatter.3.cloned.1.call-update) | async-done | bytes 65552 | tf_op jit(solution)/shard_map/reduce_scatter | solution.py:33
  109.3 0.0 copy-done.1
  109.3 0.0 copy-done.2
  109.3 1.8 multiply_convert_fusion
  111.1 0.6 multiply_reduce_fusion.1
  112.3 22.2 %reduce-scatter.5.cloned.1.call-done = bf16[32,1024]{1,0:T(8,128)(2,1)} async-done(((bf16[128,1024]{1,0:T(8,128)(2,1)}), bf16[32,1024]{1,0:T(8,128)(2,1)}) %reduce-scatter.5.cloned.1.call-update) | async-done | bytes 65552 | tf_op jit(solution)/shard_map/reduce_scatter | solution.py:39
  134.5 1.7 fusion.1
  136.2 39.3 %psum.23 = f32[]{:T(128)} all-reduce(f32[]{:T(128)S(6)} %sub.45), channel_id=1, replica_groups=mesh['row'=4,'col'=8] {'row','col'}, use_global_device_ids=true, to_apply=%region_12.0 | all-reduce | flops 1 | bytes 8 | tf_op jit(solution)/shard_map/psum | solution.py:59
  (2 shorter events, 0.0 us)
Async XLA Ops:
  7.2 10.8 %copy-start = (bf16[32,1024]{1,0:T(8,128)(2,1)S(1)}, bf16[32,1024]{1,0:T(8,128)(2,1)}, u32[]{:S(2)}) copy-start(bf16[32,1024]{1,0:T(8,128)(2,1)} %param.3) | copy-start | bytes 196612
  7.2 102.1 %reduce-scatter.3.cloned.1.call-start = ((), (), s32[]{:S(2)}) async-start(), calls=%async_computation.2 | async-start | bytes 589824 | tf_op jit(solution)/shard_map/reduce_scatter | solution.py:33
  80.9 53.6 %reduce-scatter.5.cloned.1.call-start = ((), (), s32[]{:S(2)}) async-start(), calls=%async_computation.3 | async-start | bytes 327680 | tf_op jit(solution)/shard_map/reduce_scatter | solution.py:39
  82.0 27.3 %copy-start.1 = (bf16[32,1024]{1,0:T(8,128)(2,1)S(1)}, bf16[32,1024]{1,0:T(8,128)(2,1)}, u32[]{:S(2)}) copy-start(bf16[32,1024]{1,0:T(8,128)(2,1)} %param.4) | copy-start | bytes 196612
  84.7 24.6 %copy-start.2 = (s32[1,32]{1,0:T(1,128)S(1)}, s32[1,32]{1,0:T(1,128)}, u32[]{:S(2)}) copy-start(s32[1,32]{1,0:T(1,128)} %param.5) | copy-start | bytes 388
Sparse Core Ops, SparseCore 0:
  81.0 28.2 reduce-scatter.2
  112.2 22.2 reduce-scatter.4
where the time goes:
time: 185 us; the launch traced here: 184 us
  blocking collectives  111 us (60%)
  waiting for transfers between devices  46.8 us (25%)
  between operations  17.8 us (10%)
  matrix products  6.12 us (3%)
  other arithmetic  2.16 us (1%)
    psum x1, blocking collectives, local(): summed = lax.psum(local_terms, ('row', 'col'))  39.3 us
    reduce_scatter x1, waiting for transfers between devices, local(): lax.psum_scatter(jnp.dot(weights, passage_all, preferred_element_type=jnp...  24.6 us
    reduce_scatter x1, waiting for transfers between devices, local(): lax.psum_scatter(lax.dot_general(weights, query_all, (((0,), (0,)), ((),...  22.2 us
    all_gather x1, blocking collectives, local(): query_all = lax.all_gather(query, 'col', axis=0, tiled=True)  15.4 us
    pmax x1, blocking collectives, local(): row_peak = lax.pmax(row_local_peak, 'col')  14.6 us
    psum x1, blocking collectives, local(): row_sum = lax.psum(jnp.exp(scores - row_peak[:, None]).sum(axis=1), 'col')  13.6 us
    all_gather x1, blocking collectives, local(): passage_all = lax.all_gather(passage, 'row', axis=0, tiled=True)  10.7 us
    pmax x1, blocking collectives, local(): col_peak = lax.pmax(col_local_peak, 'row')  8.93 us
  transfers between devices with their start and end apart: 2, of which 2 were waited for; matrix products, arithmetic and copies ran while one was open for 3% of the time, Pallas kernels for 0%

commit v1 on v0

v1 whole, which is shorter than its diff:
```python
import functools

import jax
import jax.numpy as jnp
from jax import lax
from jax.experimental import pallas as pl
from jax.experimental.pallas import tpu as pltpu
from jax.sharding import PartitionSpec as P

logit_scale = 20.0
MESH = pl.DeviceIdType.MESH
F32 = jnp.float32
BF16 = jnp.bfloat16
NT = (((1,), (1,)), ((), ()))
TN = (((0,), (0,)), ((), ()))


def kernel(
    n_row, n_col, q_ref, p_ref, pos_ref, loss_ref, gq_ref, gp_ref,
    q_all, p_all, pos_v, pair_p, pair_q, row_stat, col_stat,
    dq_send, dp_send, dq_recv, dp_recv, loss_g, loss_z,
    local_sem, q_ss, q_rs, p_ss, p_rs, rst_ss, rst_rs, cst_ss, cst_rs,
    dq_ss, dq_rs, dp_ss, dp_rs, lg_ss, lg_rs, lz_ss, lz_rs,
):
    rows, width = q_ref.shape
    n_z = n_col // 2
    n_g = n_row * 2
    n_q = n_z * rows
    n_p = n_g * rows
    r = lax.axis_index("row")
    c = lax.axis_index("col")
    z = c // 2
    core = c % 2
    g = r * 2 + core

    def z_dev(d):
        zz = lax.rem(z + d, n_z)
        return zz, (r, zz * 2 + core)

    def g_dev(d):
        gg = lax.rem(g + d, n_g)
        return gg, (gg // 2, z * 2 + gg % 2)

    def z_copy(d, src, dst, ss, rs):
        return pltpu.make_async_remote_copy(
            src_ref=src, dst_ref=dst, send_sem=ss.at[d], recv_sem=rs.at[d],
            device_id=z_dev(d)[1], device_id_type=MESH)

    def g_copy(d, src, dst, ss, rs):
        return pltpu.make_async_remote_copy(
            src_ref=src, dst_ref=dst, send_sem=ss.at[d], recv_sem=rs.at[d],
            device_id=g_dev(d)[1], device_id_type=MESH)

    z_range = range(1, n_z)
    g_range = range(1, n_g)

    own_p = pltpu.make_async_copy(p_ref, p_all.at[g], local_sem.at[0])
    own_q = pltpu.make_async_copy(q_ref, q_all.at[z], local_sem.at[1])
    own_pos = pltpu.make_async_copy(pos_ref, pos_v, local_sem.at[2])
    own_p.start()
    own_q.start()
    own_pos.start()

    barrier = pltpu.get_barrier_semaphore()
    for d in z_range:
        pl.semaphore_signal(barrier, inc=1, device_id=z_dev(d)[1], device_id_type=MESH)
    for d in g_range:
        pl.semaphore_signal(barrier, inc=1, device_id=g_dev(d)[1], device_id_type=MESH)
    pl.semaphore_wait(barrier, n_z - 1 + n_g - 1)

    q_copies = [z_copy(d, q_ref, q_all.at[z], q_ss, q_rs) for d in z_range]
    p_copies = [g_copy(d, p_ref, p_all.at[g], p_ss, p_rs) for d in g_range]
    for cp in q_copies:
        cp.start()
    for cp in p_copies:
        cp.start()

    own_p.wait()
    own_q.wait()
    own_pos.wait()
    q_own = q_all[z]
    p_own = p_all[g]
    slot = lax.broadcasted_iota(jnp.int32, (rows, rows), 0)
    onehot_t = jnp.where(slot == pos_v[...], 1.0, 0.0).astype(F32)
    paired_p = jnp.dot(onehot_t.T.astype(BF16), p_own, preferred_element_type=F32)
    pair_p[...] = paired_p
    pair_q[...] = jnp.dot(onehot_t.astype(BF16), q_own, preferred_element_type=F32)
    pos_sum = logit_scale * jnp.sum(q_own.astype(F32) * paired_p, axis=(0, 1), keepdims=True)

    for cp in q_copies:
        cp.wait()
    for cp in p_copies:
        cp.wait()

    q_mat = q_all[...].reshape(n_q, width)
    p_mat = p_all[...].reshape(n_p, width)
    s = logit_scale * lax.dot_general(q_mat, p_mat, NT, preferred_element_type=F32)
    s_t = logit_scale * lax.dot_general(p_mat, q_mat, NT, preferred_element_type=F32)

    col_peak = jnp.max(s, axis=0, keepdims=True)
    col_sum = jnp.sum(jnp.exp(s - col_peak), axis=0, keepdims=True)
    col_stat[g, 0:1, :] = col_peak
    col_stat[g, 1:2, :] = col_sum
    cst = [g_copy(d, col_stat.at[g], col_stat.at[g], cst_ss, cst_rs) for d in g_range]
    for cp in cst:
        cp.start()
    row_peak = jnp.max(s_t, axis=0, keepdims=True)
    row_sum = jnp.sum(jnp.exp(s_t - row_peak), axis=0, keepdims=True)
    row_stat[z, 0:1, :] = row_peak
    row_stat[z, 1:2, :] = row_sum
    row_stat[z, 2:3, :] = jnp.broadcast_to(pos_sum, (1, n_q))
    rst = [z_copy(d, row_stat.at[z], row_stat.at[z], rst_ss, rst_rs) for d in z_range]
    for cp in rst:
        cp.start()
    for cp in rst:
        cp.wait()
    for cp in cst:
        cp.wait()

    def merge(ref):
        peak = ref[:, 0, :]
        total = ref[:, 1, :]
        top = jnp.max(peak, axis=0, keepdims=True)
        return top + jnp.log(jnp.sum(total * jnp.exp(peak - top), axis=0, keepdims=True))

    row_lse = merge(row_stat)
    col_lse = merge(col_stat)
    pos_group = jnp.sum(row_stat[:, 2, 0:1], axis=0, keepdims=True)
    loss_g[g] = jnp.broadcast_to(jnp.sum(row_lse, axis=1, keepdims=True) - 2.0 * pos_group, (8, 128))
    loss_z[z] = jnp.broadcast_to(jnp.sum(col_lse, axis=1, keepdims=True), (8, 128))

    row_mat = jnp.broadcast_to(row_lse, (128, n_q)).T
    row_mat = jnp.concatenate([row_mat] * (n_p // 128), axis=1)
    w = (0.5 * (jnp.exp(s - row_mat) + jnp.exp(s - col_lse))).astype(BF16)

    dq = jnp.dot(w, p_mat, preferred_element_type=F32).astype(BF16)
    dq_send[...] = dq.reshape(n_z, rows, width)
    dqc = [z_copy(d, dq_send.at[z_dev(d)[0]], dq_recv.at[z], dq_ss, dq_rs) for d in z_range]
    lzc = [z_copy(d, loss_z.at[z], loss_z.at[z], lz_ss, lz_rs) for d in z_range]
    for cp in dqc + lzc:
        cp.start()
    dp = lax.dot_general(w, q_mat, TN, preferred_element_type=F32).astype(BF16)
    dp_send[...] = dp.reshape(n_g, rows, width)
    dpc = [g_copy(d, dp_send.at[g_dev(d)[0]], dp_recv.at[g], dp_ss, dp_rs) for d in g_range]
    lgc = [g_copy(d, loss_g.at[g], loss_g.at[g], lg_ss, lg_rs) for d in g_range]
    for cp in dpc + lgc:
        cp.start()
    dq_recv[z] = dq_send[z]
    dp_recv[g] = dp_send[g]

    for cp in lzc + lgc:
        cp.wait()
    total = jnp.sum(loss_g[:, 0, 0:1], axis=0, keepdims=True) + jnp.sum(loss_z[:, 0, 0:1], axis=0, keepdims=True)
    loss_ref[...] = total / (2.0 * rows * n_row * n_col)

    for cp in dpc:
        cp.wait()
    acc = dp_recv[0].astype(F32)
    for i in range(1, n_g):
        acc += dp_recv[i].astype(F32)
    gp_ref[...] = (logit_scale * (acc - pair_q[...])).astype(BF16)
    for cp in dqc:
        cp.wait()
    acc = dq_recv[0].astype(F32)
    for i in range(1, n_z):
        acc += dq_recv[i].astype(F32)
    gq_ref[...] = (logit_scale * (acc - pair_p[...])).astype(BF16)


def local(n_row, n_col, query, passage, positive):
    rows, width = query.shape
    n_z, n_g = n_col // 2, n_row * 2
    n_q, n_p = n_z * rows, n_g * rows
    dma = pltpu.SemaphoreType.DMA
    loss, gq, gp = pl.pallas_call(
        functools.partial(kernel, n_row, n_col),
        out_shape=(
            jax.ShapeDtypeStruct((1, 1), F32),
            jax.ShapeDtypeStruct((rows, width), BF16),
            jax.ShapeDtypeStruct((rows, width), BF16),
        ),
        in_specs=[pl.BlockSpec(memory_space=pl.ANY)] * 3,
        out_specs=[pl.BlockSpec(memory_space=pltpu.VMEM)] * 3,
        scratch_shapes=[
            pltpu.VMEM((n_z, rows, width), BF16),
            pltpu.VMEM((n_g, rows, width), BF16),
            pltpu.VMEM((1, rows), jnp.int32),
            pltpu.VMEM((rows, width), F32),
            pltpu.VMEM((rows, width), F32),
            pltpu.VMEM((n_z, 8, n_q), F32),
            pltpu.VMEM((n_g, 8, n_p), F32),
            pltpu.VMEM((n_z, rows, width), BF16),
            pltpu.VMEM((n_g, rows, width), BF16),
            pltpu.VMEM((n_z, rows, width), BF16),
            pltpu.VMEM((n_g, rows, width), BF16),
            pltpu.VMEM((n_g, 8, 128), F32),
            pltpu.VMEM((n_z, 8, 128), F32),
            dma((3,)),
            dma((n_z,)), dma((n_z,)), dma((n_g,)), dma((n_g,)),
            dma((n_z,)), dma((n_z,)), dma((n_g,)), dma((n_g,)),
            dma((n_z,)), dma((n_z,)), dma((n_g,)), dma((n_g,)),
            dma((n_g,)), dma((n_g,)), dma((n_z,)), dma((n_z,)),
        ],
        compiler_params=pltpu.CompilerParams(
            collective_id=0, has_side_effects=True, vmem_limit_bytes=48 * 1024 * 1024),
    )(query, passage, positive)
    return loss[0, 0], gq, gp


def solution(mesh):
    return jax.shard_map(
        functools.partial(local, mesh.shape["row"], mesh.shape["col"]),
        mesh=mesh,
        in_specs=(P(("row", "col"), None), P(("row", "col"), None), P(("row", "col"), None)),
        out_specs=(P(), P(("row", "col"), None), P(("row", "col"), None)),
        check_vma=False,
    )
```

time: 185 us -> 33.3 us (0.18)
  blocking collectives: 111 us -> 0 us
  waiting for transfers between devices: 46.8 us -> 0 us
  Pallas kernels: 0 us -> 27.1 us
  between operations: 17.8 us -> 2.38 us
  matrix products: 6.12 us -> 0 us
  local copies, waits for them, and re-layouts: 0.01 us -> 3.59 us
  other arithmetic: 2.16 us -> 0 us
    psum x3 -> x0, blocking collectives: 61.5 us -> none  [the longest x1 39.3 us: local(): summed = lax.psum(local_terms, ('row', 'col'))]
    reduce_scatter x2 -> x0, waiting for transfers between devices: 46.7 us -> none  [the longest x1 24.6 us: local(): lax.psum_scatter(jnp.dot(weights, passage_all, preferred_element_type=jnp...]
    pallas_call x0 -> x1, Pallas kernels: none -> 27.1 us  [local(): pl.pallas_call(functools.partial(kernel, n_row, n_col), out_shape=(jax.Sh...]
    all_gather x2 -> x0, blocking collectives: 26.1 us -> none  [the longest x1 15.4 us: local(): query_all = lax.all_gather(query, 'col', axis=0, tiled=True)]
    pmax x2 -> x0, blocking collectives: 23.5 us -> none  [the longest x1 14.6 us: local(): row_peak = lax.pmax(row_local_peak, 'col')]
    dot_general x5 -> x0, matrix products: 6.12 us -> none  [the longest x1 1.8 us: local(): jnp.dot(onehot, passage, preferred_element_type=jnp.float32)]
    unnamed x6 -> x8, local copies, waits for them, and re-layouts: 0.01 us -> 3.59 us
    reduce_sum x4 -> x0, other arithmetic: 2.14 us -> none  [the longest x1 0.67 us: local(): jnp.sum(col_part)]
  transfers between devices with their start and end apart: 2 -> 0, of which waited for: 2 -> 0; matrix products, arithmetic and copies ran while one was open for 3% -> 0% of each run, Pallas kernels for 0% -> 0%
where the time goes in v1:
time: 33.3 us; the launch traced here: 33.1 us
  Pallas kernels  27.1 us (81%)
  local copies, waits for them, and re-layouts  3.59 us (11%)
  between operations  2.38 us (7%)
    pallas_call x1, Pallas kernels, local(): pl.pallas_call(functools.partial(kernel, n_row, n_col), out_shape=(jax.Sh...  27.1 us
    unnamed x8, local copies, waits for them, and re-layouts  3.59 us

profile of v1, /device:TPU:0, one launch (start us, length us, event | category | flops | bytes accessed | tf_op | source)
XLA Modules:
  0.0 33.1 jit_solution(7284107965580194404)
XLA Ops:
  0.6 0.0 copy-start
  0.6 0.8 %copy-done = bf16[32,1024]{1,0:T(8,128)(2,1)S(1)} copy-done((bf16[32,1024]{1,0:T(8,128)(2,1)S(1)}, bf16[32,1024]{1,0:T(8,128)(2,1)}, u32[]{:S(2)}) %copy-start) | copy-done | bytes 65560
  1.5 0.0 copy-start.1
  1.5 0.8 %copy-done.1 = bf16[32,1024]{1,0:T(8,128)(2,1)S(1)} copy-done((bf16[32,1024]{1,0:T(8,128)(2,1)S(1)}, bf16[32,1024]{1,0:T(8,128)(2,1)}, u32[]{:S(2)}) %copy-start.1) | copy-done | bytes 65560
  2.3 0.0 copy-start.2
  2.3 0.7 %copy-done.2 = s32[1,32]{1,0:T(1,128)S(1)} copy-done((s32[1,32]{1,0:T(1,128)S(1)}, s32[1,32]{1,0:T(1,128)}, u32[]{:S(2)}) %copy-start.2) | copy-done | bytes 152
  3.0 27.1 %shard_map.58 = (f32[1,1]{1,0:T(1,128)}, bf16[32,1024]{1,0:T(8,128)(2,1)S(1)}, bf16[32,1024]{1,0:T(8,128)(2,1)S(1)}) custom-call(bf16[32,1024]{1,0:T(8,128)(2,1)S(1)} %copy-done, bf16[32,1024]{1,0:T(8,128)(2,1)S(1)} %copy-done.1, s32[1,32]{1,0:T(1,128)S(1)} %copy-done.2), custom_call_target="tpu_custom_call" | custom-call | tf_op jit(solution)/shard_map/pallas_call | solution.py:175
  30.7 0.6 %copy.10 = bf16[32,1024]{1,0:T(8,128)(2,1)} copy(bf16[32,1024]{1,0:T(8,128)(2,1)S(1)} %get-tuple-element.13) | data formatting | bytes 131072
  31.3 0.6 %copy.11 = bf16[32,1024]{1,0:T(8,128)(2,1)} copy(bf16[32,1024]{1,0:T(8,128)(2,1)S(1)} %get-tuple-element.14) | data formatting | bytes 131072
Async XLA Ops:
  0.6 0.8 %copy-start = (bf16[32,1024]{1,0:T(8,128)(2,1)S(1)}, bf16[32,1024]{1,0:T(8,128)(2,1)}, u32[]{:S(2)}) copy-start(bf16[32,1024]{1,0:T(8,128)(2,1)} %q_ref.1) | copy-start | bytes 196612
  1.5 0.8 %copy-start.1 = (bf16[32,1024]{1,0:T(8,128)(2,1)S(1)}, bf16[32,1024]{1,0:T(8,128)(2,1)}, u32[]{:S(2)}) copy-start(bf16[32,1024]{1,0:T(8,128)(2,1)} %p_ref.1) | copy-start | bytes 196612
  2.3 0.7 %copy-start.2 = (s32[1,32]{1,0:T(1,128)S(1)}, s32[1,32]{1,0:T(1,128)}, u32[]{:S(2)}) copy-start(s32[1,32]{1,0:T(1,128)} %pos_ref.1) | copy-start | bytes 388

commit v2 on v1

v2 whole, which is shorter than its diff:
```python
import functools

import jax
import jax.numpy as jnp
from jax import lax
from jax.experimental import pallas as pl
from jax.experimental.pallas import tpu as pltpu
from jax.sharding import PartitionSpec as P

logit_scale = 20.0
MESH = pl.DeviceIdType.MESH
F32 = jnp.float32
BF16 = jnp.bfloat16
NT = (((1,), (1,)), ((), ()))
TN = (((0,), (0,)), ((), ()))


def kernel(
    n_row, n_col, q_ref, p_ref, pos_ref, loss_ref, gq_ref, gp_ref,
    q_all, p_all, pos_v, pos_sum, pair_p, pair_q, row_stat, col_stat,
    dq_send, dp_send, dq_recv, dp_recv, loss_r, loss_z,
    local_sem, q_ss, q_rs, p_ss, p_rs, qf_ss, qf_rs, pf_ss, pf_rs, pos_ss, pos_rs,
    rst_ss, rst_rs, cst_ss, cst_rs,
    dq_ss, dq_rs, dp_ss, dp_rs, lr_ss, lr_rs, lz_ss, lz_rs,
):
    rows, width = q_ref.shape
    n_z = n_col // 2
    half_q = n_z * rows
    half_p = n_row * rows
    r = lax.axis_index("row")
    c = lax.axis_index("col")
    z = c // 2
    core = c % 2

    def z_at(d):
        return lax.rem(z + d, n_z)

    def r_at(d):
        return lax.rem(r + d, n_row)

    def z_dev(d):
        return (r, z_at(d) * 2 + core)

    def r_dev(d):
        return (r_at(d), c)

    sibling = (r, z * 2 + 1 - core)

    def copy(device, src, dst, ss, rs, i):
        return pltpu.make_async_remote_copy(
            src_ref=src, dst_ref=dst, send_sem=ss.at[i], recv_sem=rs.at[i],
            device_id=device, device_id_type=MESH)

    z_range = range(1, n_z)
    r_range = range(1, n_row)

    own_p = pltpu.make_async_copy(p_ref, p_all.at[0, r], local_sem.at[0])
    own_q = pltpu.make_async_copy(q_ref, q_all.at[0, z], local_sem.at[1])
    own_pos = pltpu.make_async_copy(pos_ref, pos_v, local_sem.at[2])
    own_p.start()
    own_q.start()
    own_pos.start()

    barrier = pltpu.get_barrier_semaphore()
    for device in [z_dev(d) for d in z_range] + [r_dev(d) for d in r_range] + [sibling]:
        pl.semaphore_signal(barrier, inc=1, device_id=device, device_id_type=MESH)
    pl.semaphore_wait(barrier, n_z + n_row - 1)

    q_copies = [copy(z_dev(d), q_ref, q_all.at[0, z], q_ss, q_rs, d) for d in z_range]
    p_copies = [copy(r_dev(d), p_ref, p_all.at[0, r], p_ss, p_rs, d) for d in r_range]
    q_shared = [copy(sibling, q_ref, q_all.at[1, z], qf_ss, qf_rs, 0)]
    p_shared = [copy(sibling, p_ref, p_all.at[1, r], pf_ss, pf_rs, 0)]
    for cp in q_copies + p_copies + q_shared + p_shared:
        cp.start()

    own_p.wait()
    own_q.wait()
    own_pos.wait()
    q_own = q_all[0, z]
    p_own = p_all[0, r]
    slot = lax.broadcasted_iota(jnp.int32, (rows, rows), 0)
    onehot_t = jnp.where(slot == pos_v[...], 1.0, 0.0).astype(F32)
    paired_p = jnp.dot(onehot_t.T.astype(BF16), p_own, preferred_element_type=F32)
    pair_p[...] = paired_p
    pair_q[...] = jnp.dot(onehot_t.astype(BF16), q_own, preferred_element_type=F32)
    own_sum = logit_scale * jnp.sum(q_own.astype(F32) * paired_p, axis=(0, 1), keepdims=True)
    pos_sum[0] = jnp.broadcast_to(own_sum, (8, 128))
    pos_copy = copy(sibling, pos_sum.at[0], pos_sum.at[1], pos_ss, pos_rs, 0)
    pos_copy.start()

    for d in r_range:
        p_copies[d - 1].wait_recv()
        at = r_at(n_row - d)
        cp = copy(sibling, p_all.at[0, at], p_all.at[1, at], pf_ss, pf_rs, d)
        cp.start()
        p_shared.append(cp)
    for d in z_range:
        q_copies[d - 1].wait_recv()
        at = z_at(n_z - d)
        cp = copy(sibling, q_all.at[0, at], q_all.at[1, at], qf_ss, qf_rs, d)
        cp.start()
        q_shared.append(cp)
    for cp in p_shared + q_shared:
        cp.wait_recv()
    pos_copy.wait()

    q_mat = q_all[...].reshape(2 * half_q, width)
    p_mat = p_all[...].reshape(2 * half_p, width)
    s = logit_scale * lax.dot_general(q_mat, p_mat, NT, preferred_element_type=F32)
    s_t = logit_scale * lax.dot_general(p_mat, q_mat, NT, preferred_element_type=F32)

    def down(x, half):
        return (jnp.sum(x[:half], axis=0, keepdims=True)
                + jnp.sum(x[half:], axis=0, keepdims=True))

    def across(x, half):
        return (jnp.sum(x[:, :half], axis=1, keepdims=True)
                + jnp.sum(x[:, half:], axis=1, keepdims=True))

    col_peak = jnp.max(s, axis=0, keepdims=True)
    col_stat[r, 0:1, :] = col_peak
    col_stat[r, 1:2, :] = down(jnp.exp(s - col_peak), half_q)
    cst = [copy(r_dev(d), col_stat.at[r], col_stat.at[r], cst_ss, cst_rs, d) for d in r_range]
    for cp in cst:
        cp.start()
    row_peak = jnp.max(s_t, axis=0, keepdims=True)
    row_stat[z, 0:1, :] = row_peak
    row_stat[z, 1:2, :] = down(jnp.exp(s_t - row_peak), half_p)
    row_stat[z, 2:3, :] = jnp.broadcast_to(pos_sum[0, 0:1, 0:1] + pos_sum[1, 0:1, 0:1], (1, 2 * half_q))
    rst = [copy(z_dev(d), row_stat.at[z], row_stat.at[z], rst_ss, rst_rs, d) for d in z_range]
    for cp in rst:
        cp.start()
    for cp in cst + rst:
        cp.wait()

    def merge(ref):
        peak = ref[:, 0, :]
        total = ref[:, 1, :]
        top = jnp.max(peak, axis=0, keepdims=True)
        return top + jnp.log(jnp.sum(total * jnp.exp(peak - top), axis=0, keepdims=True))

    row_lse = merge(row_stat)
    col_lse = merge(col_stat)
    row_mat = jnp.broadcast_to(row_lse, (128, 2 * half_q)).T
    row_mat = jnp.concatenate([row_mat] * (2 * half_p // 128), axis=1)
    w = (0.5 * (jnp.exp(s - row_mat) + jnp.exp(s - col_lse))).astype(BF16)

    dq = jnp.dot(w[:half_q], p_mat, preferred_element_type=F32).astype(BF16)
    dq_send[...] = dq.reshape(n_z, rows, width)
    dqc = [copy(z_dev(d), dq_send.at[z_at(d)], dq_recv.at[z], dq_ss, dq_rs, d) for d in z_range]
    for cp in dqc:
        cp.start()
    dp = lax.dot_general(w[:, :half_p], q_mat, TN, preferred_element_type=F32).astype(BF16)
    dp_send[...] = dp.reshape(n_row, rows, width)
    dpc = [copy(r_dev(d), dp_send.at[r_at(d)], dp_recv.at[r], dp_ss, dp_rs, d) for d in r_range]
    for cp in dpc:
        cp.start()
    pos_row = jnp.sum(row_stat[:, 2, 0:1], axis=0, keepdims=True)
    loss_r[r] = jnp.broadcast_to(across(row_lse, half_q) - 2.0 * pos_row, (8, 128))
    loss_z[z] = jnp.broadcast_to(across(col_lse, half_p), (8, 128))
    lrc = [copy(r_dev(d), loss_r.at[r], loss_r.at[r], lr_ss, lr_rs, d) for d in r_range]
    lzc = [copy(z_dev(d), loss_z.at[z], loss_z.at[z], lz_ss, lz_rs, d) for d in z_range]
    for cp in lrc + lzc:
        cp.start()
    dq_recv[z] = dq_send[z]
    dp_recv[r] = dp_send[r]
    for cp in q_copies + p_copies + q_shared + p_shared:
        cp.wait_send()

    for cp in dpc:
        cp.wait()
    acc = dp_recv[0].astype(F32)
    for i in r_range:
        acc += dp_recv[i].astype(F32)
    gp_ref[...] = (logit_scale * (acc - pair_q[...])).astype(BF16)

    for cp in lrc + lzc:
        cp.wait()
    total = jnp.sum(loss_r[:, 0, 0:1], axis=0, keepdims=True) + jnp.sum(loss_z[:, 0, 0:1], axis=0, keepdims=True)
    loss_ref[...] = total / (2.0 * rows * n_row * n_col)

    for cp in dqc:
        cp.wait()
    acc = dq_recv[0].astype(F32)
    for i in z_range:
        acc += dq_recv[i].astype(F32)
    gq_ref[...] = (logit_scale * (acc - pair_p[...])).astype(BF16)


def local(n_row, n_col, query, passage, positive):
    rows, width = query.shape
    n_z = n_col // 2
    dma = pltpu.SemaphoreType.DMA
    loss, gq, gp = pl.pallas_call(
        functools.partial(kernel, n_row, n_col),
        out_shape=(
            jax.ShapeDtypeStruct((1, 1), F32),
            jax.ShapeDtypeStruct((rows, width), BF16),
            jax.ShapeDtypeStruct((rows, width), BF16),
        ),
        in_specs=[pl.BlockSpec(memory_space=pltpu.HBM)] * 3,
        out_specs=[pl.BlockSpec(memory_space=pltpu.VMEM)] * 3,
        scratch_shapes=[
            pltpu.VMEM((2, n_z, rows, width), BF16),
            pltpu.VMEM((2, n_row, rows, width), BF16),
            pltpu.VMEM((1, rows), jnp.int32),
            pltpu.VMEM((2, 8, 128), F32),
            pltpu.VMEM((rows, width), F32),
            pltpu.VMEM((rows, width), F32),
            pltpu.VMEM((n_z, 8, 2 * n_z * rows), F32),
            pltpu.VMEM((n_row, 8, 2 * n_row * rows), F32),
            pltpu.VMEM((n_z, rows, width), BF16),
            pltpu.VMEM((n_row, rows, width), BF16),
            pltpu.VMEM((n_z, rows, width), BF16),
            pltpu.VMEM((n_row, rows, width), BF16),
            pltpu.VMEM((n_row, 8, 128), F32),
            pltpu.VMEM((n_z, 8, 128), F32),
            dma((3,)),
            dma((n_z,)), dma((n_z,)), dma((n_row,)), dma((n_row,)),
            dma((n_z,)), dma((n_z,)), dma((n_row,)), dma((n_row,)),
            dma((1,)), dma((1,)),
            dma((n_z,)), dma((n_z,)), dma((n_row,)), dma((n_row,)),
            dma((n_z,)), dma((n_z,)), dma((n_row,)), dma((n_row,)),
            dma((n_row,)), dma((n_row,)), dma((n_z,)), dma((n_z,)),
        ],
        compiler_params=pltpu.CompilerParams(
            collective_id=0, has_side_effects=True, vmem_limit_bytes=48 * 1024 * 1024),
    )(query, passage, positive)
    return loss[0, 0], gq, gp


def solution(mesh):
    return jax.shard_map(
        functools.partial(local, mesh.shape["row"], mesh.shape["col"]),
        mesh=mesh,
        in_specs=(P(("row", "col"), None), P(("row", "col"), None), P(("row", "col"), None)),
        out_specs=(P(), P(("row", "col"), None), P(("row", "col"), None)),
        check_vma=False,
    )
```

time: 33.3 us -> 32.5 us (0.976)
  Pallas kernels: 27.1 us -> 26.3 us
    pallas_call x1, Pallas kernels: 27.1 us -> 26.3 us  [local(): pl.pallas_call(functools.partial(kernel, n_row, n_col), out_shape=(jax.Sh...]
where the time goes in v2:
time: 32.5 us; the launch traced here: 32.2 us
  Pallas kernels  26.3 us (81%)
  local copies, waits for them, and re-layouts  3.59 us (11%)
  between operations  2.38 us (7%)
    pallas_call x1, Pallas kernels, local(): pl.pallas_call(functools.partial(kernel, n_row, n_col), out_shape=(jax.Sh...  26.3 us
    unnamed x8, local copies, waits for them, and re-layouts  3.59 us

profile of v2, /device:TPU:0, one launch (start us, length us, event | category | flops | bytes accessed | tf_op | source)
XLA Modules:
  0.0 32.2 jit_solution(10306008898180756872)
XLA Ops:
  0.6 0.0 copy-start
  0.6 0.8 %copy-done = bf16[32,1024]{1,0:T(8,128)(2,1)S(1)} copy-done((bf16[32,1024]{1,0:T(8,128)(2,1)S(1)}, bf16[32,1024]{1,0:T(8,128)(2,1)}, u32[]{:S(2)}) %copy-start) | copy-done | bytes 65560
  1.5 0.0 copy-start.1
  1.5 0.8 %copy-done.1 = bf16[32,1024]{1,0:T(8,128)(2,1)S(1)} copy-done((bf16[32,1024]{1,0:T(8,128)(2,1)S(1)}, bf16[32,1024]{1,0:T(8,128)(2,1)}, u32[]{:S(2)}) %copy-start.1) | copy-done | bytes 65560
  2.3 0.0 copy-start.2
  2.3 0.7 %copy-done.2 = s32[1,32]{1,0:T(1,128)S(1)} copy-done((s32[1,32]{1,0:T(1,128)S(1)}, s32[1,32]{1,0:T(1,128)}, u32[]{:S(2)}) %copy-start.2) | copy-done | bytes 152
  3.0 26.3 %shard_map.58 = (f32[1,1]{1,0:T(1,128)}, bf16[32,1024]{1,0:T(8,128)(2,1)S(1)}, bf16[32,1024]{1,0:T(8,128)(2,1)S(1)}) custom-call(bf16[32,1024]{1,0:T(8,128)(2,1)S(1)} %copy-done, bf16[32,1024]{1,0:T(8,128)(2,1)S(1)} %copy-done.1, s32[1,32]{1,0:T(1,128)S(1)} %copy-done.2), custom_call_target="tpu_custom_call" | custom-call | tf_op jit(solution)/shard_map/pallas_call | solution.py:194
  29.8 0.6 %copy.10 = bf16[32,1024]{1,0:T(8,128)(2,1)} copy(bf16[32,1024]{1,0:T(8,128)(2,1)S(1)} %get-tuple-element.13) | data formatting | bytes 131072
  30.5 0.6 %copy.11 = bf16[32,1024]{1,0:T(8,128)(2,1)} copy(bf16[32,1024]{1,0:T(8,128)(2,1)S(1)} %get-tuple-element.14) | data formatting | bytes 131072
Async XLA Ops:
  0.6 0.8 %copy-start = (bf16[32,1024]{1,0:T(8,128)(2,1)S(1)}, bf16[32,1024]{1,0:T(8,128)(2,1)}, u32[]{:S(2)}) copy-start(bf16[32,1024]{1,0:T(8,128)(2,1)} %q_ref.1) | copy-start | bytes 196612
  1.5 0.8 %copy-start.1 = (bf16[32,1024]{1,0:T(8,128)(2,1)S(1)}, bf16[32,1024]{1,0:T(8,128)(2,1)}, u32[]{:S(2)}) copy-start(bf16[32,1024]{1,0:T(8,128)(2,1)} %p_ref.1) | copy-start | bytes 196612
  2.3 0.7 %copy-start.2 = (s32[1,32]{1,0:T(1,128)S(1)}, s32[1,32]{1,0:T(1,128)}, u32[]{:S(2)}) copy-start(s32[1,32]{1,0:T(1,128)} %pos_ref.1) | copy-start | bytes 388

commit v3 on v2

--- a/solution.py
+++ b/solution.py
@@ -225,7 +225,7 @@
         ],
         compiler_params=pltpu.CompilerParams(
             collective_id=0, has_side_effects=True, vmem_limit_bytes=48 * 1024 * 1024),
-    )(query, passage, positive)
+    )(*(pltpu.with_memory_space_constraint(x, pltpu.HBM) for x in (query, passage, positive)))
     return loss[0, 0], gq, gp
 
 

time: 32.5 us -> 30.1 us (0.926)
  local copies, waits for them, and re-layouts: 3.59 us -> 1.26 us
    unnamed x8 -> x2, local copies, waits for them, and re-layouts: 3.59 us -> 1.26 us
where the time goes in v3:
time: 30.1 us; the launch traced here: 30 us
  Pallas kernels  26.4 us (88%)
  between operations  2.33 us (8%)
  local copies, waits for them, and re-layouts  1.26 us (4%)
    pallas_call x1, Pallas kernels, local(): pl.pallas_call(functools.partial(kernel, n_row, n_col), out_shape=(jax.Sh...  26.4 us
    unnamed x2, local copies, waits for them, and re-layouts  1.26 us

profile of v3, /device:TPU:0, one launch (start us, length us, event | category | flops | bytes accessed | tf_op | source)
XLA Modules:
  0.0 30.0 jit_solution(17141138147394383332)
XLA Ops:
  0.6 26.4 %shard_map.58 = (f32[1,1]{1,0:T(1,128)}, bf16[32,1024]{1,0:T(8,128)(2,1)S(1)}, bf16[32,1024]{1,0:T(8,128)(2,1)S(1)}) custom-call(bf16[32,1024]{1,0:T(8,128)(2,1)} %q_ref.1, bf16[32,1024]{1,0:T(8,128)(2,1)} %p_ref.1, s32[1,32]{1,0:T(1,128)} %pos_ref.1), custom_call_target="tpu_custom_call" | custom-call | tf_op jit(solution)/shard_map/pallas_call | solution.py:194
  27.6 0.6 %copy.10 = bf16[32,1024]{1,0:T(8,128)(2,1)} copy(bf16[32,1024]{1,0:T(8,128)(2,1)S(1)} %get-tuple-element.13) | data formatting | bytes 131072
  28.2 0.6 %copy.11 = bf16[32,1024]{1,0:T(8,128)(2,1)} copy(bf16[32,1024]{1,0:T(8,128)(2,1)S(1)} %get-tuple-element.14) | data formatting | bytes 131072

commit v4 on v3

--- a/solution.py
+++ b/solution.py
@@ -177,7 +177,7 @@
     for cp in lrc + lzc:
         cp.wait()
     total = jnp.sum(loss_r[:, 0, 0:1], axis=0, keepdims=True) + jnp.sum(loss_z[:, 0, 0:1], axis=0, keepdims=True)
-    loss_ref[...] = total / (2.0 * rows * n_row * n_col)
+    loss_ref[...] = jnp.broadcast_to(total / (2.0 * rows * n_row * n_col), (8, 128))
 
     for cp in dqc:
         cp.wait()
@@ -185,6 +185,16 @@
     for i in z_range:
         acc += dq_recv[i].astype(F32)
     gq_ref[...] = (logit_scale * (acc - pair_p[...])).astype(BF16)
+
+
+def hand_out(loss_ref, gq_ref, gp_ref, loss_out, gq_out, gp_out, loss_v, sem):
+    loss_v[...] = loss_ref[0:1, 0:1]
+    pairs = ((gq_ref, gq_out), (gp_ref, gp_out), (loss_v, loss_out))
+    copies = [pltpu.make_async_copy(src, dst, sem.at[i]) for i, (src, dst) in enumerate(pairs)]
+    for cp in copies:
+        cp.start()
+    for cp in copies:
+        cp.wait()
 
 
 def local(n_row, n_col, query, passage, positive):
@@ -194,7 +204,7 @@
     loss, gq, gp = pl.pallas_call(
         functools.partial(kernel, n_row, n_col),
         out_shape=(
-            jax.ShapeDtypeStruct((1, 1), F32),
+            jax.ShapeDtypeStruct((8, 128), F32),
             jax.ShapeDtypeStruct((rows, width), BF16),
             jax.ShapeDtypeStruct((rows, width), BF16),
         ),
@@ -226,6 +236,17 @@
         compiler_params=pltpu.CompilerParams(
             collective_id=0, has_side_effects=True, vmem_limit_bytes=48 * 1024 * 1024),
     )(*(pltpu.with_memory_space_constraint(x, pltpu.HBM) for x in (query, passage, positive)))
+    loss, gq, gp = pl.pallas_call(
+        hand_out,
+        out_shape=(
+            jax.ShapeDtypeStruct((1, 1), F32),
+            jax.ShapeDtypeStruct(gq.shape, BF16),
+            jax.ShapeDtypeStruct(gp.shape, BF16),
+        ),
+        in_specs=[pl.BlockSpec(memory_space=pltpu.VMEM)] * 3,
+        out_specs=[pl.BlockSpec(memory_space=pl.ANY)] * 3,
+        scratch_shapes=[pltpu.VMEM((1, 1), F32), dma((3,))],
+    )(loss, gq, gp)
     return loss[0, 0], gq, gp
 
 

time: 30.1 us -> 30.2 us (level)
  between operations: 2.33 us -> 0.65 us
  Pallas kernels: 26.4 us -> 27.5 us
  local copies, waits for them, and re-layouts: 1.26 us -> 1.83 us
    pallas_call x0 -> x1, Pallas kernels: none -> 1.55 us  [local(): pl.pallas_call(hand_out, out_shape=(jax.ShapeDtypeStruct((1, 1), F32), ja...]
    unnamed x2 -> x6, local copies, waits for them, and re-layouts: 1.26 us -> 1.83 us
    pallas_call x1, Pallas kernels: 26.4 us -> 26 us  [local(): pl.pallas_call(functools.partial(kernel, n_row, n_col), out_shape=(jax.Sh...]
where the time goes in v4:
time: 30.2 us; the launch traced here: 30 us
  Pallas kernels  27.5 us (91%)
  local copies, waits for them, and re-layouts  1.83 us (6%)
  between operations  0.65 us (2%)
    pallas_call x1, Pallas kernels, local(): pl.pallas_call(functools.partial(kernel, n_row, n_col), out_shape=(jax.Sh...  26 us
    unnamed x6, local copies, waits for them, and re-layouts  1.83 us
    pallas_call x1, Pallas kernels, local(): pl.pallas_call(hand_out, out_shape=(jax.ShapeDtypeStruct((1, 1), F32), ja...  1.55 us

profile of v4, /device:TPU:0, one launch (start us, length us, event | category | flops | bytes accessed | tf_op | source)
XLA Modules:
  0.0 30.0 jit_solution(7805349925277203270)
XLA Ops:
  0.6 26.0 %shard_map.58 = (f32[8,128]{1,0:T(8,128)S(1)}, bf16[32,1024]{1,0:T(8,128)(2,1)S(1)}, bf16[32,1024]{1,0:T(8,128)(2,1)S(1)}) custom-call(bf16[32,1024]{1,0:T(8,128)(2,1)} %q_ref.1, bf16[32,1024]{1,0:T(8,128)(2,1)} %p_ref.1, s32[1,32]{1,0:T(1,128)} %pos_ref.1), custom_call_target="tpu_custom_call" | custom-call | tf_op jit(solution)/shard_map/pallas_call | solution.py:204
  26.6 0.0 copy-start
  26.6 0.6 %copy-done = bf16[32,1024]{1,0:T(8,128)(2,1)} copy-done((bf16[32,1024]{1,0:T(8,128)(2,1)}, bf16[32,1024]{1,0:T(8,128)(2,1)S(1)}, u32[]{:S(2)}) %copy-start) | copy-done | bytes 65560
  27.2 0.0 copy-start.1
  27.2 0.6 %copy-done.1 = bf16[32,1024]{1,0:T(8,128)(2,1)} copy-done((bf16[32,1024]{1,0:T(8,128)(2,1)}, bf16[32,1024]{1,0:T(8,128)(2,1)S(1)}, u32[]{:S(2)}) %copy-start.1) | copy-done | bytes 65560
  27.9 0.0 copy-start.2
  27.9 0.6 %copy-done.2 = f32[8,128]{1,0:T(8,128)} copy-done((f32[8,128]{1,0:T(8,128)}, f32[8,128]{1,0:T(8,128)S(1)}, u32[]{:S(2)}) %copy-start.2) | copy-done | bytes 4120
  28.4 1.6 %shard_map.59 = (f32[1,1]{1,0:T(1,128)}, bf16[32,1024]{1,0:T(8,128)(2,1)}, bf16[32,1024]{1,0:T(8,128)(2,1)}) custom-call(f32[8,128]{1,0:T(8,128)} %copy-done.2, bf16[32,1024]{1,0:T(8,128)(2,1)} %copy-done, bf16[32,1024]{1,0:T(8,128)(2,1)} %copy-done.1), custom_call_target="tpu_custom_call" | custom-call | tf_op jit(solution)/shard_map/pallas_call | solution.py:239
Async XLA Ops:
  26.6 0.6 %copy-start = (bf16[32,1024]{1,0:T(8,128)(2,1)}, bf16[32,1024]{1,0:T(8,128)(2,1)S(1)}, u32[]{:S(2)}) copy-start(bf16[32,1024]{1,0:T(8,128)(2,1)S(1)} %get-tuple-element.10.gq_ref) | copy-start | bytes 196612
  27.2 0.6 %copy-start.1 = (bf16[32,1024]{1,0:T(8,128)(2,1)}, bf16[32,1024]{1,0:T(8,128)(2,1)S(1)}, u32[]{:S(2)}) copy-start(bf16[32,1024]{1,0:T(8,128)(2,1)S(1)} %get-tuple-element.11.gp_ref) | copy-start | bytes 196612
  27.9 0.6 %copy-start.2 = (f32[8,128]{1,0:T(8,128)}, f32[8,128]{1,0:T(8,128)S(1)}, u32[]{:S(2)}) copy-start(f32[8,128]{1,0:T(8,128)S(1)} %get-tuple-element.9.loss_ref) | copy-start | bytes 12292

commit v5 on v3

--- a/solution.py
+++ b/solution.py
@@ -18,7 +18,7 @@
 def kernel(
     n_row, n_col, q_ref, p_ref, pos_ref, loss_ref, gq_ref, gp_ref,
     q_all, p_all, pos_v, pos_sum, pair_p, pair_q, row_stat, col_stat,
-    dq_send, dp_send, dq_recv, dp_recv, loss_r, loss_z,
+    dq_send, dp_send, dq_recv, dp_recv, dq_relay, loss_r, loss_z, gq_v, gp_v, loss_v,
     local_sem, q_ss, q_rs, p_ss, p_rs, qf_ss, qf_rs, pf_ss, pf_rs, pos_ss, pos_rs,
     rst_ss, rst_rs, cst_ss, cst_rs,
     dq_ss, dq_rs, dp_ss, dp_rs, lr_ss, lr_rs, lz_ss, lz_rs,
@@ -51,7 +51,24 @@
             src_ref=src, dst_ref=dst, send_sem=ss.at[i], recv_sem=rs.at[i],
             device_id=device, device_id_type=MESH)
 
+    relayed = n_z >= 4
+    last = n_z - 1
     z_range = range(1, n_z)
+    z_order = list(z_range)
+    if relayed:
+        inner = [2] + ([n_z - 2] if n_z > 4 else []) + list(range(3, n_z - 2))
+        low = z < n_z // 2
+        z_order = inner + [jnp.where(low, last, 1), jnp.where(low, 1, last)]
+
+    def crosses(d):
+        return ((z == 0) & (d == last)) | ((z == last) & (d == 1))
+
+    def unless_crossing(d, action):
+        if relayed and not (isinstance(d, int) and 1 < d < last):
+            pl.when(jnp.logical_not(crosses(d)))(action)
+        else:
+            action()
+
     r_range = range(1, n_row)
 
     own_p = pltpu.make_async_copy(p_ref, p_all.at[0, r], local_sem.at[0])
@@ -66,11 +83,13 @@
         pl.semaphore_signal(barrier, inc=1, device_id=device, device_id_type=MESH)
     pl.semaphore_wait(barrier, n_z + n_row - 1)
 
-    q_copies = [copy(z_dev(d), q_ref, q_all.at[0, z], q_ss, q_rs, d) for d in z_range]
+    q_copies = [copy(z_dev(d), q_ref, q_all.at[0, z], q_ss, q_rs, d) for d in z_order]
     p_copies = [copy(r_dev(d), p_ref, p_all.at[0, r], p_ss, p_rs, d) for d in r_range]
     q_shared = [copy(sibling, q_ref, q_all.at[1, z], qf_ss, qf_rs, 0)]
     p_shared = [copy(sibling, p_ref, p_all.at[1, r], pf_ss, pf_rs, 0)]
-    for cp in q_copies + p_copies + q_shared + p_shared:
+    for d, cp in zip(z_order, q_copies):
+        unless_crossing(d, cp.start)
+    for cp in p_copies + q_shared + p_shared:
         cp.start()
 
     own_p.wait()
@@ -88,18 +107,37 @@
     pos_copy = copy(sibling, pos_sum.at[0], pos_sum.at[1], pos_ss, pos_rs, 0)
     pos_copy.start()
 
+    def share_q(i):
+        d = z_order[i]
+        at = z_at(n_z - d)
+        cp = copy(sibling, q_all.at[0, at], q_all.at[1, at], qf_ss, qf_rs, d)
+        cp.start()
+        q_shared.append(cp)
+
+    first_q = 0
+    if relayed:
+        to_last = pltpu.make_async_remote_copy(
+            src_ref=q_all.at[0, 0], dst_ref=q_all.at[0, 0], send_sem=q_ss.at[0], recv_sem=q_rs.at[last],
+            device_id=z_dev(1), device_id_type=MESH)
+        to_first = pltpu.make_async_remote_copy(
+            src_ref=q_all.at[0, last], dst_ref=q_all.at[0, last], send_sem=q_ss.at[0], recv_sem=q_rs.at[1],
+            device_id=z_dev(last), device_id_type=MESH)
+        first_q = 1 if n_z == 4 else 2
+        for i in range(first_q):
+            q_copies[i].wait_recv()
+        pl.when(z == n_z - 2)(to_last.start)
+        pl.when(z == 1)(to_first.start)
+        for i in range(first_q):
+            share_q(i)
     for d in r_range:
         p_copies[d - 1].wait_recv()
         at = r_at(n_row - d)
         cp = copy(sibling, p_all.at[0, at], p_all.at[1, at], pf_ss, pf_rs, d)
         cp.start()
         p_shared.append(cp)
-    for d in z_range:
-        q_copies[d - 1].wait_recv()
-        at = z_at(n_z - d)
-        cp = copy(sibling, q_all.at[0, at], q_all.at[1, at], qf_ss, qf_rs, d)
-        cp.start()
-        q_shared.append(cp)
+    for i in range(first_q, n_z - 1):
+        q_copies[i].wait_recv()
+        share_q(i)
     for cp in p_shared + q_shared:
         cp.wait_recv()
     pos_copy.wait()
@@ -147,14 +185,36 @@
 
     dq = jnp.dot(w[:half_q], p_mat, preferred_element_type=F32).astype(BF16)
     dq_send[...] = dq.reshape(n_z, rows, width)
-    dqc = [copy(z_dev(d), dq_send.at[z_at(d)], dq_recv.at[z], dq_ss, dq_rs, d) for d in z_range]
-    for cp in dqc:
-        cp.start()
+    dqc = [copy(z_dev(d), dq_send.at[z_at(d)], dq_recv.at[z], dq_ss, dq_rs, d) for d in z_order]
+    if relayed:
+        up = copy(z_dev(1), dq_send.at[last], dq_relay, dq_ss, dq_rs, 0)
+        down_ = copy(z_dev(last), dq_send.at[0], dq_relay, dq_ss, dq_rs, 0)
+        pl.when(z == 0)(up.start)
+        pl.when(z == last)(down_.start)
+        adds = (z == 1) | (z == n_z - 2)
+        far = jnp.where(z == 1, last, 0)
+    for d, cp in zip(z_order, dqc):
+        if relayed:
+            target = z_at(d)
+            goes_late = adds & (target == far)
+            pl.when(jnp.logical_not(crosses(d) | goes_late))(cp.start)
+        else:
+            cp.start()
     dp = lax.dot_general(w[:, :half_p], q_mat, TN, preferred_element_type=F32).astype(BF16)
     dp_send[...] = dp.reshape(n_row, rows, width)
     dpc = [copy(r_dev(d), dp_send.at[r_at(d)], dp_recv.at[r], dp_ss, dp_rs, d) for d in r_range]
     for cp in dpc:
         cp.start()
+    if relayed:
+        @pl.when(adds)
+        def _():
+            up.wait_recv()
+            dq_send[far] = (dq_send[far].astype(F32) + dq_relay[...].astype(F32)).astype(BF16)
+            copy(z_dev(far - z + n_z), dq_send.at[far], dq_recv.at[z], dq_ss, dq_rs, lax.rem(far - z + n_z, n_z)).start()
+
+        @pl.when((z == 0) | (z == last))
+        def _():
+            dq_recv[last - z] = jnp.zeros((rows, width), BF16)
     pos_row = jnp.sum(row_stat[:, 2, 0:1], axis=0, keepdims=True)
     loss_r[r] = jnp.broadcast_to(across(row_lse, half_q) - 2.0 * pos_row, (8, 128))
     loss_z[z] = jnp.broadcast_to(across(col_lse, half_p), (8, 128))
@@ -164,7 +224,12 @@
         cp.start()
     dq_recv[z] = dq_send[z]
     dp_recv[r] = dp_send[r]
-    for cp in q_copies + p_copies + q_shared + p_shared:
+    for d, cp in zip(z_order, q_copies):
+        unless_crossing(d, cp.wait_send)
+    if relayed:
+        pl.when(z == n_z - 2)(to_last.wait_send)
+        pl.when(z == 1)(to_first.wait_send)
+    for cp in p_copies + q_shared + p_shared:
         cp.wait_send()
 
     for cp in dpc:
@@ -172,19 +237,43 @@
     acc = dp_recv[0].astype(F32)
     for i in r_range:
         acc += dp_recv[i].astype(F32)
-    gp_ref[...] = (logit_scale * (acc - pair_q[...])).astype(BF16)
+    gp_v[...] = (logit_scale * (acc - pair_q[...])).astype(BF16)
+    gp_out = pltpu.make_async_copy(gp_v, gp_ref, local_sem.at[3])
+    gp_out.start()
 
     for cp in lrc + lzc:
         cp.wait()
     total = jnp.sum(loss_r[:, 0, 0:1], axis=0, keepdims=True) + jnp.sum(loss_z[:, 0, 0:1], axis=0, keepdims=True)
-    loss_ref[...] = total / (2.0 * rows * n_row * n_col)
-
-    for cp in dqc:
-        cp.wait()
+    loss_v[...] = total / (2.0 * rows * n_row * n_col)
+    loss_out = pltpu.make_async_copy(loss_v, loss_ref, local_sem.at[4])
+    loss_out.start()
+
+    if relayed:
+        pl.when((z == 0) | (z == last))(up.wait_send)
+    for d, cp in zip(z_order, dqc):
+        unless_crossing(d, cp.wait_send)
+        if relayed:
+            from_far = ((z == 0) & (d == 1)) | ((z == last) & (d == last))
+            pl.when(jnp.logical_not(from_far))(cp.wait_recv)
+        else:
+            cp.wait_recv()
     acc = dq_recv[0].astype(F32)
     for i in z_range:
         acc += dq_recv[i].astype(F32)
-    gq_ref[...] = (logit_scale * (acc - pair_p[...])).astype(BF16)
+    gq_v[...] = (logit_scale * (acc - pair_p[...])).astype(BF16)
+    gq_out = pltpu.make_async_copy(gq_v, gq_ref, local_sem.at[5])
+    gq_out.start()
+    for cp in (gp_out, loss_out, gq_out):
+        cp.wait()
+
+
+def hand_out(*refs):
+    *arrays, sem = refs
+    copies = [pltpu.make_async_copy(arrays[i], arrays[i + 3], sem.at[i]) for i in range(3)]
+    for cp in copies:
+        cp.start()
+    for cp in copies:
+        cp.wait()
 
 
 def local(n_row, n_col, query, passage, positive):
@@ -194,12 +283,12 @@
     loss, gq, gp = pl.pallas_call(
         functools.partial(kernel, n_row, n_col),
         out_shape=(
-            jax.ShapeDtypeStruct((1, 1), F32),
-            jax.ShapeDtypeStruct((rows, width), BF16),
-            jax.ShapeDtypeStruct((rows, width), BF16),
+            pltpu.HBM((1, 1), F32),
+            pltpu.HBM((rows, width), BF16),
+            pltpu.HBM((rows, width), BF16),
         ),
         in_specs=[pl.BlockSpec(memory_space=pltpu.HBM)] * 3,
-        out_specs=[pl.BlockSpec(memory_space=pltpu.VMEM)] * 3,
+        out_specs=[pl.BlockSpec(memory_space=pltpu.HBM)] * 3,
         scratch_shapes=[
             pltpu.VMEM((2, n_z, rows, width), BF16),
             pltpu.VMEM((2, n_row, rows, width), BF16),
@@ -213,9 +302,13 @@
             pltpu.VMEM((n_row, rows, width), BF16),
             pltpu.VMEM((n_z, rows, width), BF16),
             pltpu.VMEM((n_row, rows, width), BF16),
+            pltpu.VMEM((rows, width), BF16),
             pltpu.VMEM((n_row, 8, 128), F32),
             pltpu.VMEM((n_z, 8, 128), F32),
-            dma((3,)),
+            pltpu.VMEM((rows, width), BF16),
+            pltpu.VMEM((rows, width), BF16),
+            pltpu.VMEM((1, 1), F32),
+            dma((6,)),
             dma((n_z,)), dma((n_z,)), dma((n_row,)), dma((n_row,)),
             dma((n_z,)), dma((n_z,)), dma((n_row,)), dma((n_row,)),
             dma((1,)), dma((1,)),
@@ -226,6 +319,14 @@
         compiler_params=pltpu.CompilerParams(
             collective_id=0, has_side_effects=True, vmem_limit_bytes=48 * 1024 * 1024),
     )(*(pltpu.with_memory_space_constraint(x, pltpu.HBM) for x in (query, passage, positive)))
+    results = (loss, gq, gp)
+    loss, gq, gp = pl.pallas_call(
+        hand_out,
+        out_shape=tuple(jax.ShapeDtypeStruct(x.shape, x.dtype) for x in results),
+        in_specs=[pl.BlockSpec(memory_space=pltpu.HBM)] * 3,
+        out_specs=[pl.BlockSpec(memory_space=pltpu.HBM)] * 3,
+        scratch_shapes=[dma((3,))],
+    )(*(pltpu.with_memory_space_constraint(x, pltpu.HBM) for x in results))
     return loss[0, 0], gq, gp
 
 

time: 30.1 us -> 33.7 us (1.12)
  Pallas kernels: 26.4 us -> 32.9 us
  between operations: 2.33 us -> 0.64 us
  local copies, waits for them, and re-layouts: 1.26 us -> 0 us
    pallas_call x1 -> x2, Pallas kernels: 26.4 us -> 32.9 us  [the longest x1 27.2 us: local(): pl.pallas_call(functools.partial(kernel, n_row, n_col), out_shape=(pltpu....]
    unnamed x2 -> x0, local copies, waits for them, and re-layouts: 1.26 us -> none
where the time goes in v5:
time: 33.7 us; the launch traced here: 33.5 us
  Pallas kernels  32.9 us (98%)
  between operations  0.64 us (2%)
    pallas_call x1, Pallas kernels, local(): pl.pallas_call(functools.partial(kernel, n_row, n_col), out_shape=(pltpu....  27.2 us
    pallas_call x1, Pallas kernels, local(): pl.pallas_call(hand_out, out_shape=tuple((jax.ShapeDtypeStruct(x.shape, x...  5.72 us

profile of v5, /device:TPU:0, one launch (start us, length us, event | category | flops | bytes accessed | tf_op | source)
XLA Modules:
  0.0 33.5 jit_solution(14712592201923318464)
XLA Ops:
  0.6 27.2 %shard_map.58 = (f32[1,1]{1,0:T(1,128)}, bf16[32,1024]{1,0:T(8,128)(2,1)}, bf16[32,1024]{1,0:T(8,128)(2,1)}) custom-call(bf16[32,1024]{1,0:T(8,128)(2,1)} %q_ref.1, bf16[32,1024]{1,0:T(8,128)(2,1)} %p_ref.1, s32[1,32]{1,0:T(1,128)} %pos_ref.1), custom_call_target="tpu_custom_call" | custom-call | tf_op jit(solution)/shard_map/pallas_call | solution.py:283
  27.8 5.7 %shard_map.59 = (f32[1,1]{1,0:T(1,128)}, bf16[32,1024]{1,0:T(8,128)(2,1)}, bf16[32,1024]{1,0:T(8,128)(2,1)}) custom-call(f32[1,1]{1,0:T(1,128)} %get-tuple-element.9.refs_0_, bf16[32,1024]{1,0:T(8,128)(2,1)} %get-tuple-element.10.refs_1_, bf16[32,1024]{1,0:T(8,128)(2,1)} %get-tuple-element.11.refs_2_), custom_call_target="tpu_custom_call" | custom-call | tf_op jit(solution)/shard_map/pallas_call | solution.py:323

commit v6 on v4

--- a/solution.py
+++ b/solution.py
@@ -107,7 +107,6 @@
     q_mat = q_all[...].reshape(2 * half_q, width)
     p_mat = p_all[...].reshape(2 * half_p, width)
     s = logit_scale * lax.dot_general(q_mat, p_mat, NT, preferred_element_type=F32)
-    s_t = logit_scale * lax.dot_general(p_mat, q_mat, NT, preferred_element_type=F32)
 
     def down(x, half):
         return (jnp.sum(x[:half], axis=0, keepdims=True)
@@ -117,18 +116,21 @@
         return (jnp.sum(x[:, :half], axis=1, keepdims=True)
                 + jnp.sum(x[:, half:], axis=1, keepdims=True))
 
+    row_peak = jnp.max(s, axis=1, keepdims=True)
+    row_exp = jnp.exp(s - row_peak)
+    row_sum = across(row_exp, half_p)
+    lane = lax.broadcasted_iota(jnp.int32, (2 * half_q, 128), 1)
+    pair_sum = pos_sum[0, 0:1, 0:1] + pos_sum[1, 0:1, 0:1]
+    row_stat[z] = jnp.where(lane == 0, row_peak, jnp.where(lane == 1, row_sum, pair_sum)).T[0:8]
+    rst = [copy(z_dev(d), row_stat.at[z], row_stat.at[z], rst_ss, rst_rs, d) for d in z_range]
+    for cp in rst:
+        cp.start()
     col_peak = jnp.max(s, axis=0, keepdims=True)
+    col_exp = jnp.exp(s - col_peak)
     col_stat[r, 0:1, :] = col_peak
-    col_stat[r, 1:2, :] = down(jnp.exp(s - col_peak), half_q)
+    col_stat[r, 1:2, :] = down(col_exp, half_q)
     cst = [copy(r_dev(d), col_stat.at[r], col_stat.at[r], cst_ss, cst_rs, d) for d in r_range]
     for cp in cst:
-        cp.start()
-    row_peak = jnp.max(s_t, axis=0, keepdims=True)
-    row_stat[z, 0:1, :] = row_peak
-    row_stat[z, 1:2, :] = down(jnp.exp(s_t - row_peak), half_p)
-    row_stat[z, 2:3, :] = jnp.broadcast_to(pos_sum[0, 0:1, 0:1] + pos_sum[1, 0:1, 0:1], (1, 2 * half_q))
-    rst = [copy(z_dev(d), row_stat.at[z], row_stat.at[z], rst_ss, rst_rs, d) for d in z_range]
-    for cp in rst:
         cp.start()
     for cp in cst + rst:
         cp.wait()
@@ -141,9 +143,11 @@
 
     row_lse = merge(row_stat)
     col_lse = merge(col_stat)
-    row_mat = jnp.broadcast_to(row_lse, (128, 2 * half_q)).T
+    row_factor = 0.5 * jnp.exp(row_stat[z, 0:1, :] - row_lse)
+    row_mat = jnp.broadcast_to(row_factor, (128, 2 * half_q)).T
     row_mat = jnp.concatenate([row_mat] * (2 * half_p // 128), axis=1)
-    w = (0.5 * (jnp.exp(s - row_mat) + jnp.exp(s - col_lse))).astype(BF16)
+    col_factor = 0.5 * jnp.exp(col_peak - col_lse)
+    w = (row_exp * row_mat + col_exp * col_factor).astype(BF16)
 
     dq = jnp.dot(w[:half_q], p_mat, preferred_element_type=F32).astype(BF16)
     dq_send[...] = dq.reshape(n_z, rows, width)
@@ -204,9 +208,9 @@
     loss, gq, gp = pl.pallas_call(
         functools.partial(kernel, n_row, n_col),
         out_shape=(
-            jax.ShapeDtypeStruct((8, 128), F32),
-            jax.ShapeDtypeStruct((rows, width), BF16),
-            jax.ShapeDtypeStruct((rows, width), BF16),
+            pltpu.VMEM((8, 128), F32),
+            pltpu.VMEM((rows, width), BF16),
+            pltpu.VMEM((rows, width), BF16),
         ),
         in_specs=[pl.BlockSpec(memory_space=pltpu.HBM)] * 3,
         out_specs=[pl.BlockSpec(memory_space=pltpu.VMEM)] * 3,
@@ -246,7 +250,7 @@
         in_specs=[pl.BlockSpec(memory_space=pltpu.VMEM)] * 3,
         out_specs=[pl.BlockSpec(memory_space=pl.ANY)] * 3,
         scratch_shapes=[pltpu.VMEM((1, 1), F32), dma((3,))],
-    )(loss, gq, gp)
+    )(*(pltpu.with_memory_space_constraint(x, pltpu.VMEM) for x in (loss, gq, gp)))
     return loss[0, 0], gq, gp
 
 

time: 30.2 us -> 27.6 us (0.914)
  local copies, waits for them, and re-layouts: 1.83 us -> 0 us
  Pallas kernels: 27.5 us -> 26.8 us
    unnamed x6 -> x0, local copies, waits for them, and re-layouts: 1.83 us -> none
    pallas_call x1, Pallas kernels: 1.55 us -> 0.68 us  [local(): pl.pallas_call(hand_out, out_shape=(jax.ShapeDtypeStruct((1, 1), F32), ja...]
where the time goes in v6:
time: 27.6 us; the launch traced here: 27.4 us
  Pallas kernels  26.8 us (97%)
  between operations  0.64 us (2%)
    pallas_call x1, Pallas kernels, local(): pl.pallas_call(functools.partial(kernel, n_row, n_col), out_shape=(pltpu....  26.1 us
    pallas_call x1, Pallas kernels, local(): pl.pallas_call(hand_out, out_shape=(jax.ShapeDtypeStruct((1, 1), F32), ja...  0.68 us

profile of v6, /device:TPU:0, one launch (start us, length us, event | category | flops | bytes accessed | tf_op | source)
XLA Modules:
  0.0 27.4 jit_solution(8187191859142412764)
XLA Ops:
  0.6 26.1 %shard_map.58 = (f32[8,128]{1,0:T(8,128)S(1)}, bf16[32,1024]{1,0:T(8,128)(2,1)S(1)}, bf16[32,1024]{1,0:T(8,128)(2,1)S(1)}) custom-call(bf16[32,1024]{1,0:T(8,128)(2,1)} %q_ref.1, bf16[32,1024]{1,0:T(8,128)(2,1)} %p_ref.1, s32[1,32]{1,0:T(1,128)} %pos_ref.1), custom_call_target="tpu_custom_call" | custom-call | tf_op jit(solution)/shard_map/pallas_call | solution.py:208
  26.7 0.7 %shard_map.59 = (f32[1,1]{1,0:T(1,128)}, bf16[32,1024]{1,0:T(8,128)(2,1)}, bf16[32,1024]{1,0:T(8,128)(2,1)}) custom-call(f32[8,128]{1,0:T(8,128)S(1)} %get-tuple-element.9.loss_ref, bf16[32,1024]{1,0:T(8,128)(2,1)S(1)} %get-tuple-element.10.gq_ref, bf16[32,1024]{1,0:T(8,128)(2,1)S(1)} %get-tuple-element.11.gp_ref), custom_call_target="tpu_custom_call" | custom-call | tf_op jit(solution)/shard_map/pallas_call | solution.py:243

commit v7 on v6

--- a/solution.py
+++ b/solution.py
@@ -19,6 +19,7 @@
     n_row, n_col, q_ref, p_ref, pos_ref, loss_ref, gq_ref, gp_ref,
     q_all, p_all, pos_v, pos_sum, pair_p, pair_q, row_stat, col_stat,
     dq_send, dp_send, dq_recv, dp_recv, loss_r, loss_z,
+    s_v, row_exp, col_exp, stat_cols, w_q, w_p,
     local_sem, q_ss, q_rs, p_ss, p_rs, qf_ss, qf_rs, pf_ss, pf_rs, pos_ss, pos_rs,
     rst_ss, rst_rs, cst_ss, cst_rs,
     dq_ss, dq_rs, dp_ss, dp_rs, lr_ss, lr_rs, lz_ss, lz_rs,
@@ -27,6 +28,9 @@
     n_z = n_col // 2
     half_q = n_z * rows
     half_p = n_row * rows
+    n_q, n_p = 2 * half_q, 2 * half_p
+    step = 256
+    block = 64
     r = lax.axis_index("row")
     c = lax.axis_index("col")
     z = c // 2
@@ -76,14 +80,21 @@
     own_p.wait()
     own_q.wait()
     own_pos.wait()
-    q_own = q_all[0, z]
-    p_own = p_all[0, r]
     slot = lax.broadcasted_iota(jnp.int32, (rows, rows), 0)
     onehot_t = jnp.where(slot == pos_v[...], 1.0, 0.0).astype(F32)
-    paired_p = jnp.dot(onehot_t.T.astype(BF16), p_own, preferred_element_type=F32)
-    pair_p[...] = paired_p
-    pair_q[...] = jnp.dot(onehot_t.astype(BF16), q_own, preferred_element_type=F32)
-    own_sum = logit_scale * jnp.sum(q_own.astype(F32) * paired_p, axis=(0, 1), keepdims=True)
+    by_query = onehot_t.T.astype(BF16)
+    by_passage = onehot_t.astype(BF16)
+
+    def pair_step(i, total):
+        cols = pl.ds(pl.multiple_of(i * step, step), step)
+        q_part = q_all[0, z, :, cols]
+        paired = jnp.dot(by_query, p_all[0, r, :, cols], preferred_element_type=F32)
+        pair_p[:, cols] = paired
+        pair_q[:, cols] = jnp.dot(by_passage, q_part, preferred_element_type=F32)
+        return total + q_part.astype(F32) * paired
+
+    products = lax.fori_loop(0, width // step, pair_step, jnp.zeros((rows, step), F32))
+    own_sum = logit_scale * jnp.sum(products, axis=(0, 1), keepdims=True)
     pos_sum[0] = jnp.broadcast_to(own_sum, (8, 128))
     pos_copy = copy(sibling, pos_sum.at[0], pos_sum.at[1], pos_ss, pos_rs, 0)
     pos_copy.start()
@@ -104,31 +115,59 @@
         cp.wait_recv()
     pos_copy.wait()
 
-    q_mat = q_all[...].reshape(2 * half_q, width)
-    p_mat = p_all[...].reshape(2 * half_p, width)
-    s = logit_scale * lax.dot_general(q_mat, p_mat, NT, preferred_element_type=F32)
-
-    def down(x, half):
-        return (jnp.sum(x[:half], axis=0, keepdims=True)
-                + jnp.sum(x[half:], axis=0, keepdims=True))
+    def score_step(i, carry):
+        cols = pl.ds(pl.multiple_of(i * step, step), step)
+        part = lax.dot_general(
+            q_all[:, :, :, cols].reshape(n_q, step), p_all[:, :, :, cols].reshape(n_p, step),
+            NT, preferred_element_type=F32)
+
+        @pl.when(i == 0)
+        def _():
+            s_v[...] = part
+
+        @pl.when(i > 0)
+        def _():
+            s_v[...] += part
+        return carry
+
+    lax.fori_loop(0, width // step, score_step, 0)
 
     def across(x, half):
         return (jnp.sum(x[:, :half], axis=1, keepdims=True)
                 + jnp.sum(x[:, half:], axis=1, keepdims=True))
 
-    row_peak = jnp.max(s, axis=1, keepdims=True)
-    row_exp = jnp.exp(s - row_peak)
-    row_sum = across(row_exp, half_p)
-    lane = lax.broadcasted_iota(jnp.int32, (2 * half_q, 128), 1)
+    lane = lax.broadcasted_iota(jnp.int32, (block, 128), 1)
     pair_sum = pos_sum[0, 0:1, 0:1] + pos_sum[1, 0:1, 0:1]
-    row_stat[z] = jnp.where(lane == 0, row_peak, jnp.where(lane == 1, row_sum, pair_sum)).T[0:8]
+
+    def row_step(i, peak):
+        at = pl.ds(pl.multiple_of(i * block, block), block)
+        x = logit_scale * s_v[at, :]
+        s_v[at, :] = x
+        row_peak = jnp.max(x, axis=1, keepdims=True)
+        e = jnp.exp(x - row_peak)
+        row_exp[at, :] = e
+        row_sum = across(e, half_p)
+        stat_cols[at, :] = jnp.where(lane == 0, row_peak, jnp.where(lane == 1, row_sum, pair_sum))
+        return jnp.maximum(peak, jnp.max(x, axis=0, keepdims=True))
+
+    col_peak = lax.fori_loop(0, n_q // block, row_step, jnp.full((1, n_p), -jnp.inf, F32))
+    row_stat[z] = stat_cols[...].T[0:8]
     rst = [copy(z_dev(d), row_stat.at[z], row_stat.at[z], rst_ss, rst_rs, d) for d in z_range]
     for cp in rst:
         cp.start()
-    col_peak = jnp.max(s, axis=0, keepdims=True)
-    col_exp = jnp.exp(s - col_peak)
+
+    def col_step(i, total):
+        at = pl.ds(pl.multiple_of(i * block, block), block)
+        e = jnp.exp(s_v[at, :] - col_peak)
+        col_exp[at, :] = e
+        return total + jnp.sum(e, axis=0, keepdims=True)
+
+    per_half = half_q // block
+    zero = jnp.zeros((1, n_p), F32)
+    col_sum = (lax.fori_loop(0, per_half, col_step, zero)
+               + lax.fori_loop(per_half, 2 * per_half, col_step, zero))
     col_stat[r, 0:1, :] = col_peak
-    col_stat[r, 1:2, :] = down(col_exp, half_q)
+    col_stat[r, 1:2, :] = col_sum
     cst = [copy(r_dev(d), col_stat.at[r], col_stat.at[r], cst_ss, cst_rs, d) for d in r_range]
     for cp in cst:
         cp.start()
@@ -144,18 +183,37 @@
     row_lse = merge(row_stat)
     col_lse = merge(col_stat)
     row_factor = 0.5 * jnp.exp(row_stat[z, 0:1, :] - row_lse)
-    row_mat = jnp.broadcast_to(row_factor, (128, 2 * half_q)).T
-    row_mat = jnp.concatenate([row_mat] * (2 * half_p // 128), axis=1)
+    stat_cols[...] = jnp.broadcast_to(row_factor, (128, n_q)).T
     col_factor = 0.5 * jnp.exp(col_peak - col_lse)
-    w = (row_exp * row_mat + col_exp * col_factor).astype(BF16)
-
-    dq = jnp.dot(w[:half_q], p_mat, preferred_element_type=F32).astype(BF16)
-    dq_send[...] = dq.reshape(n_z, rows, width)
+
+    def weight_step(i, carry):
+        at = pl.ds(pl.multiple_of(i * block, block), block)
+        factor = jnp.concatenate([stat_cols[at, :]] * (n_p // 128), axis=1)
+        s_v[at, :] = row_exp[at, :] * factor + col_exp[at, :] * col_factor
+        return carry
+
+    lax.fori_loop(0, n_q // block, weight_step, 0)
+    w_q[...] = s_v[0:half_q, :].astype(BF16)
+    w_p[...] = s_v[:, 0:half_p].T.astype(BF16)
+
+    def dq_step(i, carry):
+        cols = pl.ds(pl.multiple_of(i * step, step), step)
+        dq = jnp.dot(w_q[...], p_all[:, :, :, cols].reshape(n_p, step), preferred_element_type=F32)
+        dq_send[:, :, cols] = dq.astype(BF16).reshape(n_z, rows, step)
+        return carry
+
+    lax.fori_loop(0, width // step, dq_step, 0)
     dqc = [copy(z_dev(d), dq_send.at[z_at(d)], dq_recv.at[z], dq_ss, dq_rs, d) for d in z_range]
     for cp in dqc:
         cp.start()
-    dp = lax.dot_general(w[:, :half_p], q_mat, TN, preferred_element_type=F32).astype(BF16)
-    dp_send[...] = dp.reshape(n_row, rows, width)
+
+    def dp_step(i, carry):
+        cols = pl.ds(pl.multiple_of(i * step, step), step)
+        dp = jnp.dot(w_p[...], q_all[:, :, :, cols].reshape(n_q, step), preferred_element_type=F32)
+        dp_send[:, :, cols] = dp.astype(BF16).reshape(n_row, rows, step)
+        return carry
+
+    lax.fori_loop(0, width // step, dp_step, 0)
     dpc = [copy(r_dev(d), dp_send.at[r_at(d)], dp_recv.at[r], dp_ss, dp_rs, d) for d in r_range]
     for cp in dpc:
         cp.start()
@@ -173,10 +231,17 @@
 
     for cp in dpc:
         cp.wait()
-    acc = dp_recv[0].astype(F32)
-    for i in r_range:
-        acc += dp_recv[i].astype(F32)
-    gp_ref[...] = (logit_scale * (acc - pair_q[...])).astype(BF16)
+    def add_up(terms, paired, out, count):
+        def body(i, carry):
+            cols = pl.ds(pl.multiple_of(i * step, step), step)
+            acc = terms[0, :, cols].astype(F32)
+            for j in range(1, count):
+                acc += terms[j, :, cols].astype(F32)
+            out[:, cols] = (logit_scale * (acc - paired[:, cols])).astype(BF16)
+            return carry
+        lax.fori_loop(0, width // step, body, 0)
+
+    add_up(dp_recv, pair_q, gp_ref, n_row)
 
     for cp in lrc + lzc:
         cp.wait()
@@ -185,10 +250,7 @@
 
     for cp in dqc:
         cp.wait()
-    acc = dq_recv[0].astype(F32)
-    for i in z_range:
-        acc += dq_recv[i].astype(F32)
-    gq_ref[...] = (logit_scale * (acc - pair_p[...])).astype(BF16)
+    add_up(dq_recv, pair_p, gq_ref, n_z)
 
 
 def hand_out(loss_ref, gq_ref, gp_ref, loss_out, gq_out, gp_out, loss_v, sem):
@@ -204,6 +266,7 @@
 def local(n_row, n_col, query, passage, positive):
     rows, width = query.shape
     n_z = n_col // 2
+    n_q, n_p = 2 * n_z * rows, 2 * n_row * rows
     dma = pltpu.SemaphoreType.DMA
     loss, gq, gp = pl.pallas_call(
         functools.partial(kernel, n_row, n_col),
@@ -229,6 +292,12 @@
             pltpu.VMEM((n_row, rows, width), BF16),
             pltpu.VMEM((n_row, 8, 128), F32),
             pltpu.VMEM((n_z, 8, 128), F32),
+            pltpu.VMEM((n_q, n_p), F32),
+            pltpu.VMEM((n_q, n_p), F32),
+            pltpu.VMEM((n_q, n_p), F32),
+            pltpu.VMEM((n_q, 128), F32),
+            pltpu.VMEM((n_q // 2, n_p), BF16),
+            pltpu.VMEM((n_p // 2, n_q), BF16),
             dma((3,)),
             dma((n_z,)), dma((n_z,)), dma((n_row,)), dma((n_row,)),
             dma((n_z,)), dma((n_z,)), dma((n_row,)), dma((n_row,)),

time: 27.6 us -> 29.3 us (1.062)
  Pallas kernels: 26.8 us -> 28.6 us
    pallas_call x1, Pallas kernels: 26.1 us -> 27.9 us  [local(): pl.pallas_call(functools.partial(kernel, n_row, n_col), out_shape=(pltpu....]
where the time goes in v7:
time: 29.3 us; the launch traced here: 29.2 us
  Pallas kernels  28.6 us (98%)
  between operations  0.64 us (2%)
    pallas_call x1, Pallas kernels, local(): pl.pallas_call(functools.partial(kernel, n_row, n_col), out_shape=(pltpu....  27.9 us
    pallas_call x1, Pallas kernels, local(): pl.pallas_call(hand_out, out_shape=(jax.ShapeDtypeStruct((1, 1), F32), ja...  0.68 us

profile of v7, /device:TPU:0, one launch (start us, length us, event | category | flops | bytes accessed | tf_op | source)
XLA Modules:
  0.0 29.2 jit_solution(4917204885443586569)
XLA Ops:
  0.6 27.9 %shard_map.58 = (f32[8,128]{1,0:T(8,128)S(1)}, bf16[32,1024]{1,0:T(8,128)(2,1)S(1)}, bf16[32,1024]{1,0:T(8,128)(2,1)S(1)}) custom-call(bf16[32,1024]{1,0:T(8,128)(2,1)} %q_ref.1, bf16[32,1024]{1,0:T(8,128)(2,1)} %p_ref.1, s32[1,32]{1,0:T(1,128)} %pos_ref.1), custom_call_target="tpu_custom_call" | custom-call | tf_op jit(solution)/shard_map/pallas_call | solution.py:271
  28.5 0.7 %shard_map.59 = (f32[1,1]{1,0:T(1,128)}, bf16[32,1024]{1,0:T(8,128)(2,1)}, bf16[32,1024]{1,0:T(8,128)(2,1)}) custom-call(f32[8,128]{1,0:T(8,128)S(1)} %get-tuple-element.9.loss_ref, bf16[32,1024]{1,0:T(8,128)(2,1)S(1)} %get-tuple-element.10.gq_ref, bf16[32,1024]{1,0:T(8,128)(2,1)S(1)} %get-tuple-element.11.gp_ref), custom_call_target="tpu_custom_call" | custom-call | tf_op jit(solution)/shard_map/pallas_call | solution.py:312

commit v8 on v6

--- a/solution.py
+++ b/solution.py
@@ -17,9 +17,9 @@
 
 def kernel(
     n_row, n_col, q_ref, p_ref, pos_ref, loss_ref, gq_ref, gp_ref,
-    q_all, p_all, pos_v, pos_sum, pair_p, pair_q, row_stat, col_stat,
+    q_all, p_all, pos_v, pair_p, pair_q, row_stat, col_stat, col_swap, w_sent, w_got,
     dq_send, dp_send, dq_recv, dp_recv, loss_r, loss_z,
-    local_sem, q_ss, q_rs, p_ss, p_rs, qf_ss, qf_rs, pf_ss, pf_rs, pos_ss, pos_rs,
+    local_sem, q_ss, q_rs, p_ss, p_rs, qf_ss, qf_rs, pf_ss, pf_rs, w_ss, w_rs,
     rst_ss, rst_rs, cst_ss, cst_rs,
     dq_ss, dq_rs, dp_ss, dp_rs, lr_ss, lr_rs, lz_ss, lz_rs,
 ):
@@ -31,6 +31,8 @@
     c = lax.axis_index("col")
     z = c // 2
     core = c % 2
+    g = r * 2 + core
+    n_g = n_row * 2
 
     def z_at(d):
         return lax.rem(z + d, n_z)
@@ -43,6 +45,10 @@
 
     def r_dev(d):
         return (r_at(d), c)
+
+    def g_dev(d):
+        gg = lax.rem(g + d, n_g)
+        return (gg // 2, z * 2 + gg % 2)
 
     sibling = (r, z * 2 + 1 - core)
 
@@ -53,6 +59,7 @@
 
     z_range = range(1, n_z)
     r_range = range(1, n_row)
+    g_range = range(1, n_g)
 
     own_p = pltpu.make_async_copy(p_ref, p_all.at[0, r], local_sem.at[0])
     own_q = pltpu.make_async_copy(q_ref, q_all.at[0, z], local_sem.at[1])
@@ -62,15 +69,14 @@
     own_pos.start()
 
     barrier = pltpu.get_barrier_semaphore()
-    for device in [z_dev(d) for d in z_range] + [r_dev(d) for d in r_range] + [sibling]:
+    for device in [z_dev(d) for d in z_range] + [g_dev(d) for d in g_range]:
         pl.semaphore_signal(barrier, inc=1, device_id=device, device_id_type=MESH)
-    pl.semaphore_wait(barrier, n_z + n_row - 1)
+    pl.semaphore_wait(barrier, n_z - 1 + n_g - 1)
 
     q_copies = [copy(z_dev(d), q_ref, q_all.at[0, z], q_ss, q_rs, d) for d in z_range]
     p_copies = [copy(r_dev(d), p_ref, p_all.at[0, r], p_ss, p_rs, d) for d in r_range]
-    q_shared = [copy(sibling, q_ref, q_all.at[1, z], qf_ss, qf_rs, 0)]
     p_shared = [copy(sibling, p_ref, p_all.at[1, r], pf_ss, pf_rs, 0)]
-    for cp in q_copies + p_copies + q_shared + p_shared:
+    for cp in q_copies + p_copies + p_shared:
         cp.start()
 
     own_p.wait()
@@ -84,54 +90,49 @@
     pair_p[...] = paired_p
     pair_q[...] = jnp.dot(onehot_t.astype(BF16), q_own, preferred_element_type=F32)
     own_sum = logit_scale * jnp.sum(q_own.astype(F32) * paired_p, axis=(0, 1), keepdims=True)
-    pos_sum[0] = jnp.broadcast_to(own_sum, (8, 128))
-    pos_copy = copy(sibling, pos_sum.at[0], pos_sum.at[1], pos_ss, pos_rs, 0)
-    pos_copy.start()
-
     for d in r_range:
         p_copies[d - 1].wait_recv()
         at = r_at(n_row - d)
         cp = copy(sibling, p_all.at[0, at], p_all.at[1, at], pf_ss, pf_rs, d)
         cp.start()
         p_shared.append(cp)
-    for d in z_range:
-        q_copies[d - 1].wait_recv()
-        at = z_at(n_z - d)
-        cp = copy(sibling, q_all.at[0, at], q_all.at[1, at], qf_ss, qf_rs, d)
-        cp.start()
-        q_shared.append(cp)
-    for cp in p_shared + q_shared:
+    for cp in p_shared:
         cp.wait_recv()
-    pos_copy.wait()
-
-    q_mat = q_all[...].reshape(2 * half_q, width)
+    for cp in q_copies:
+        cp.wait_recv()
+
+    q_mat = q_all[0].reshape(half_q, width)
     p_mat = p_all[...].reshape(2 * half_p, width)
     s = logit_scale * lax.dot_general(q_mat, p_mat, NT, preferred_element_type=F32)
 
-    def down(x, half):
-        return (jnp.sum(x[:half], axis=0, keepdims=True)
-                + jnp.sum(x[half:], axis=0, keepdims=True))
+    s_t = logit_scale * lax.dot_general(p_mat, q_mat, NT, preferred_element_type=F32)
 
     def across(x, half):
         return (jnp.sum(x[:, :half], axis=1, keepdims=True)
                 + jnp.sum(x[:, half:], axis=1, keepdims=True))
 
-    row_peak = jnp.max(s, axis=1, keepdims=True)
-    row_exp = jnp.exp(s - row_peak)
-    row_sum = across(row_exp, half_p)
-    lane = lax.broadcasted_iota(jnp.int32, (2 * half_q, 128), 1)
-    pair_sum = pos_sum[0, 0:1, 0:1] + pos_sum[1, 0:1, 0:1]
-    row_stat[z] = jnp.where(lane == 0, row_peak, jnp.where(lane == 1, row_sum, pair_sum)).T[0:8]
+    row_peak = jnp.max(s_t, axis=0, keepdims=True)
+    row_stat[z, 0:1, :] = row_peak
+    row_stat[z, 1:2, :] = jnp.sum(jnp.exp(s_t - row_peak), axis=0, keepdims=True)
+    row_stat[z, 2:3, :] = jnp.broadcast_to(own_sum, (1, half_q))
     rst = [copy(z_dev(d), row_stat.at[z], row_stat.at[z], rst_ss, rst_rs, d) for d in z_range]
     for cp in rst:
         cp.start()
     col_peak = jnp.max(s, axis=0, keepdims=True)
     col_exp = jnp.exp(s - col_peak)
-    col_stat[r, 0:1, :] = col_peak
-    col_stat[r, 1:2, :] = down(col_exp, half_q)
-    cst = [copy(r_dev(d), col_stat.at[r], col_stat.at[r], cst_ss, cst_rs, d) for d in r_range]
+    col_sum = jnp.sum(col_exp, axis=0, keepdims=True)
+    col_stat[g, 0:1, :] = col_peak
+    col_stat[g, 1:2, :] = col_sum
+    col_swap[0:1, :half_p] = col_peak[:, half_p:]
+    col_swap[0:1, half_p:] = col_peak[:, :half_p]
+    col_swap[1:2, :half_p] = col_sum[:, half_p:]
+    col_swap[1:2, half_p:] = col_sum[:, :half_p]
+    cst = [copy(g_dev(d), col_swap if d % 2 else col_stat.at[g], col_stat.at[g], cst_ss, cst_rs, d)
+           for d in g_range]
     for cp in cst:
         cp.start()
+    q_shared = copy(sibling, q_all.at[0], q_all.at[1], qf_ss, qf_rs, 0)
+    q_shared.start()
     for cp in cst + rst:
         cp.wait()
 
@@ -143,32 +144,39 @@
 
     row_lse = merge(row_stat)
     col_lse = merge(col_stat)
-    row_factor = 0.5 * jnp.exp(row_stat[z, 0:1, :] - row_lse)
-    row_mat = jnp.broadcast_to(row_factor, (128, 2 * half_q)).T
+    row_mat = jnp.broadcast_to(row_lse, (128, half_q)).T
     row_mat = jnp.concatenate([row_mat] * (2 * half_p // 128), axis=1)
     col_factor = 0.5 * jnp.exp(col_peak - col_lse)
-    w = (row_exp * row_mat + col_exp * col_factor).astype(BF16)
-
-    dq = jnp.dot(w[:half_q], p_mat, preferred_element_type=F32).astype(BF16)
+    w = 0.5 * jnp.exp(s - row_mat) + col_exp * col_factor
+    w_t = w.T.astype(BF16)
+    w_sent[...] = w_t[half_p:]
+    w_copy = copy(sibling, w_sent, w_got, w_ss, w_rs, 0)
+    w_copy.start()
+
+    dq = jnp.dot(w.astype(BF16), p_mat, preferred_element_type=F32).astype(BF16)
     dq_send[...] = dq.reshape(n_z, rows, width)
     dqc = [copy(z_dev(d), dq_send.at[z_at(d)], dq_recv.at[z], dq_ss, dq_rs, d) for d in z_range]
     for cp in dqc:
         cp.start()
-    dp = lax.dot_general(w[:, :half_p], q_mat, TN, preferred_element_type=F32).astype(BF16)
+    q_shared.wait()
+    w_copy.wait()
+    w_both = jnp.concatenate([w_t[:half_p], w_got[...]], axis=1)
+    q_both = q_all[...].reshape(2 * half_q, width)
+    dp = jnp.dot(w_both, q_both, preferred_element_type=F32).astype(BF16)
     dp_send[...] = dp.reshape(n_row, rows, width)
     dpc = [copy(r_dev(d), dp_send.at[r_at(d)], dp_recv.at[r], dp_ss, dp_rs, d) for d in r_range]
     for cp in dpc:
         cp.start()
     pos_row = jnp.sum(row_stat[:, 2, 0:1], axis=0, keepdims=True)
-    loss_r[r] = jnp.broadcast_to(across(row_lse, half_q) - 2.0 * pos_row, (8, 128))
+    loss_r[g] = jnp.broadcast_to(jnp.sum(row_lse, axis=1, keepdims=True) - 2.0 * pos_row, (8, 128))
     loss_z[z] = jnp.broadcast_to(across(col_lse, half_p), (8, 128))
-    lrc = [copy(r_dev(d), loss_r.at[r], loss_r.at[r], lr_ss, lr_rs, d) for d in r_range]
+    lrc = [copy(g_dev(d), loss_r.at[g], loss_r.at[g], lr_ss, lr_rs, d) for d in g_range]
     lzc = [copy(z_dev(d), loss_z.at[z], loss_z.at[z], lz_ss, lz_rs, d) for d in z_range]
     for cp in lrc + lzc:
         cp.start()
     dq_recv[z] = dq_send[z]
     dp_recv[r] = dp_send[r]
-    for cp in q_copies + p_copies + q_shared + p_shared:
+    for cp in q_copies + p_copies + p_shared:
         cp.wait_send()
 
     for cp in dpc:
@@ -203,7 +211,7 @@
 
 def local(n_row, n_col, query, passage, positive):
     rows, width = query.shape
-    n_z = n_col // 2
+    n_z, n_g = n_col // 2, n_row * 2
     dma = pltpu.SemaphoreType.DMA
     loss, gq, gp = pl.pallas_call(
         functools.partial(kernel, n_row, n_col),
@@ -218,24 +226,26 @@
             pltpu.VMEM((2, n_z, rows, width), BF16),
             pltpu.VMEM((2, n_row, rows, width), BF16),
             pltpu.VMEM((1, rows), jnp.int32),
-            pltpu.VMEM((2, 8, 128), F32),
             pltpu.VMEM((rows, width), F32),
             pltpu.VMEM((rows, width), F32),
-            pltpu.VMEM((n_z, 8, 2 * n_z * rows), F32),
-            pltpu.VMEM((n_row, 8, 2 * n_row * rows), F32),
+            pltpu.VMEM((n_z, 8, n_z * rows), F32),
+            pltpu.VMEM((n_g, 8, n_g * rows), F32),
+            pltpu.VMEM((8, n_g * rows), F32),
+            pltpu.VMEM((n_row * rows, n_z * rows), BF16),
+            pltpu.VMEM((n_row * rows, n_z * rows), BF16),
             pltpu.VMEM((n_z, rows, width), BF16),
             pltpu.VMEM((n_row, rows, width), BF16),
             pltpu.VMEM((n_z, rows, width), BF16),
             pltpu.VMEM((n_row, rows, width), BF16),
-            pltpu.VMEM((n_row, 8, 128), F32),
+            pltpu.VMEM((n_g, 8, 128), F32),
             pltpu.VMEM((n_z, 8, 128), F32),
             dma((3,)),
             dma((n_z,)), dma((n_z,)), dma((n_row,)), dma((n_row,)),
+            dma((1,)), dma((1,)), dma((n_row,)), dma((n_row,)),
+            dma((1,)), dma((1,)),
+            dma((n_z,)), dma((n_z,)), dma((n_g,)), dma((n_g,)),
             dma((n_z,)), dma((n_z,)), dma((n_row,)), dma((n_row,)),
-            dma((1,)), dma((1,)),
-            dma((n_z,)), dma((n_z,)), dma((n_row,)), dma((n_row,)),
-            dma((n_z,)), dma((n_z,)), dma((n_row,)), dma((n_row,)),
-            dma((n_row,)), dma((n_row,)), dma((n_z,)), dma((n_z,)),
+            dma((n_g,)), dma((n_g,)), dma((n_z,)), dma((n_z,)),
         ],
         compiler_params=pltpu.CompilerParams(
             collective_id=0, has_side_effects=True, vmem_limit_bytes=48 * 1024 * 1024),

time: 27.6 us -> 27.1 us (0.982)
  Pallas kernels: 26.8 us -> 26.3 us
    pallas_call x1, Pallas kernels: 26.1 us -> 25.6 us  [local(): pl.pallas_call(functools.partial(kernel, n_row, n_col), out_shape=(pltpu....]
where the time goes in v8:
time: 27.1 us; the launch traced here: 26.9 us
  Pallas kernels  26.3 us (97%)
  between operations  0.64 us (2%)
    pallas_call x1, Pallas kernels, local(): pl.pallas_call(functools.partial(kernel, n_row, n_col), out_shape=(pltpu....  25.6 us
    pallas_call x1, Pallas kernels, local(): pl.pallas_call(hand_out, out_shape=(jax.ShapeDtypeStruct((1, 1), F32), ja...  0.68 us

profile of v8, /device:TPU:0, one launch (start us, length us, event | category | flops | bytes accessed | tf_op | source)
XLA Modules:
  0.0 26.9 jit_solution(6543316450135360822)
XLA Ops:
  0.6 25.6 %shard_map.58 = (f32[8,128]{1,0:T(8,128)S(1)}, bf16[32,1024]{1,0:T(8,128)(2,1)S(1)}, bf16[32,1024]{1,0:T(8,128)(2,1)S(1)}) custom-call(bf16[32,1024]{1,0:T(8,128)(2,1)} %q_ref.1, bf16[32,1024]{1,0:T(8,128)(2,1)} %p_ref.1, s32[1,32]{1,0:T(1,128)} %pos_ref.1), custom_call_target="tpu_custom_call" | custom-call | tf_op jit(solution)/shard_map/pallas_call | solution.py:216
  26.3 0.7 %shard_map.59 = (f32[1,1]{1,0:T(1,128)}, bf16[32,1024]{1,0:T(8,128)(2,1)}, bf16[32,1024]{1,0:T(8,128)(2,1)}) custom-call(f32[8,128]{1,0:T(8,128)S(1)} %get-tuple-element.9.loss_ref, bf16[32,1024]{1,0:T(8,128)(2,1)S(1)} %get-tuple-element.10.gq_ref, bf16[32,1024]{1,0:T(8,128)(2,1)S(1)} %get-tuple-element.11.gp_ref), custom_call_target="tpu_custom_call" | custom-call | tf_op jit(solution)/shard_map/pallas_call | solution.py:253

commit v9 on v8

--- a/solution.py
+++ b/solution.py
@@ -76,7 +76,7 @@
     q_copies = [copy(z_dev(d), q_ref, q_all.at[0, z], q_ss, q_rs, d) for d in z_range]
     p_copies = [copy(r_dev(d), p_ref, p_all.at[0, r], p_ss, p_rs, d) for d in r_range]
     p_shared = [copy(sibling, p_ref, p_all.at[1, r], pf_ss, pf_rs, 0)]
-    for cp in q_copies + p_copies + p_shared:
+    for cp in p_copies + q_copies + p_shared:
         cp.start()
 
     own_p.wait()

time: 27.1 us -> 27.1 us (level)
  no operation moved by 1% of the time
where the time goes in v9:
time: 27.1 us; the launch traced here: 26.9 us
  Pallas kernels  26.3 us (97%)
  between operations  0.64 us (2%)
    pallas_call x1, Pallas kernels, local(): pl.pallas_call(functools.partial(kernel, n_row, n_col), out_shape=(pltpu....  25.6 us
    pallas_call x1, Pallas kernels, local(): pl.pallas_call(hand_out, out_shape=(jax.ShapeDtypeStruct((1, 1), F32), ja...  0.68 us

profile of v9, /device:TPU:0, one launch (start us, length us, event | category | flops | bytes accessed | tf_op | source)
XLA Modules:
  0.0 26.9 jit_solution(11586941062883532548)
XLA Ops:
  0.6 25.6 %shard_map.58 = (f32[8,128]{1,0:T(8,128)S(1)}, bf16[32,1024]{1,0:T(8,128)(2,1)S(1)}, bf16[32,1024]{1,0:T(8,128)(2,1)S(1)}) custom-call(bf16[32,1024]{1,0:T(8,128)(2,1)} %q_ref.1, bf16[32,1024]{1,0:T(8,128)(2,1)} %p_ref.1, s32[1,32]{1,0:T(1,128)} %pos_ref.1), custom_call_target="tpu_custom_call" | custom-call | tf_op jit(solution)/shard_map/pallas_call | solution.py:216
  26.3 0.7 %shard_map.59 = (f32[1,1]{1,0:T(1,128)}, bf16[32,1024]{1,0:T(8,128)(2,1)}, bf16[32,1024]{1,0:T(8,128)(2,1)}) custom-call(f32[8,128]{1,0:T(8,128)S(1)} %get-tuple-element.9.loss_ref, bf16[32,1024]{1,0:T(8,128)(2,1)S(1)} %get-tuple-element.10.gq_ref, bf16[32,1024]{1,0:T(8,128)(2,1)S(1)} %get-tuple-element.11.gp_ref), custom_call_target="tpu_custom_call" | custom-call | tf_op jit(solution)/shard_map/pallas_call | solution.py:253
